TPU v7x, 256 devices: a whole 4x4x8 slice. The times are simulated.
256 devices in a mesh: expert: 32 (over x_hi, z, core), shard: 8 (over x_lo, y).
Axes of the slice: x: 4 (x_hi: 2, x_lo: 2; x = x_hi * 2 + x_lo), y: 4, z: 8, core: 2. Of those that a mesh axis runs over, the one named last changes fastest.
Arguments:
- train_acts: bfloat16 [65536, 2048], P(('expert', 'shard')), may hold values from -6 to 6
- train_grads: bfloat16 [65536, 768], P(('expert', 'shard')), may hold values from -6 to 6
- slot_counts: int32 [256, 2, 32], P(('expert', 'shard')), may hold values from 1 to 4, as said below
- query_acts: bfloat16 [2, 32, 64, 2048], P(None, 'expert'), may hold values from -6 to 6
- query_grads: bfloat16 [2, 32, 64, 768], P(None, 'expert'), may hold values from -6 to 6
- query_ids: int32 [2, 32, 64], P(None, 'expert'), may hold values from 0 to 7
- basis_in: bfloat16 [2, 32, 2048, 2048], P(None, 'expert', None, 'shard'), may hold values from -0.125 to 0.125
- eigen_vals: bfloat16 [2, 32, 768, 2048], P(None, 'expert', None, 'shard'), may hold values from 0.5 to 8
- basis_out: bfloat16 [2, 32, 768, 768], P(None, 'expert'), may hold values from -0.21875 to 0.21875
Outputs:
- influence: float32 [8, 65536], P(None, ('expert', 'shard'))
Inputs may be any that keep to these rules, and one draw needn't show every extreme that they name: `slot_counts`: in every turn one expert has all 4 slots live from every device group.
All inputs are finite; a program needn't handle non-finite values.
Results may differ from a plain program's by a relative error of at most 0.0055.
Values may be sent and summed in bfloat16 or wider, within the bound.
No kernel may reach another device: no remote copies, remote signals or barrier semaphores. Data moves between devices by JAX's collectives and lax.ppermute only.
A program may use at most 192 MiB of HBM per device.

v0:
```python
import functools
import math

import jax
import jax.numpy as jnp
from jax import lax
from jax.experimental import pallas as pl
from jax.experimental.pallas import tpu as pltpu
from jax.sharding import Mesh, PartitionSpec as P

HIDDEN_SIZE = 2048
INNER = 768
QUERIES = 8
SLOTS = 4
TURNS = 2
DAMPING = 0.05

SIZES = (2, 8, 2, 2, 4)
AXES = ("xh", "z", "core", "xl", "y")


def flat_index(xh, z, core, xl, y):
    return (((xh * 8 + z) * 2 + core) * 2 + xl) * 4 + y


def route_groups():
    groups = []
    for core in range(2):
        for low in range(2):
            turn_y = (low, 3 - low)
            groups.append(
                [
                    flat_index(xh, z, core, xl, turn_y[k])
                    for k in range(2)
                    for xh in range(2)
                    for z in range(8)
                    for xl in range(2)
                ]
            )
    return groups


def moves(home_step, guest_step):
    pairs = []
    for core in range(2):
        for xl in range(2):
            for y in range(4):
                step = home_step if core == xl else guest_step
                if step is not None:
                    pairs.append(((core * 2 + xl) * 4 + y, step(core, xl, y)))
    return pairs


def place(core, xl, y):
    return (core * 2 + xl) * 4 + y


def cross_step(core, xl, y):
    return place(1 - core, 1 - xl, y)


def outer_step(core, xl, y):
    return place(core, xl, 3 - y)


def inner_step(core, xl, y):
    return place(core, xl, y ^ 1)


def send(x, home_step, guest_step):
    return lax.ppermute(x, ("core", "xl", "y"), moves(home_step, guest_step))


def other_core(x):
    return lax.ppermute(x, "core", [(0, 1), (1, 0)])


def rotate_kernel(rows_a, rows_b, b_out, u_ref):
    for n, rows in enumerate((rows_a, rows_b)):
        u_ref[pl.ds(n * 256, 256), :] = jnp.dot(
            rows[:, HIDDEN_SIZE:], b_out[...], preferred_element_type=jnp.float32
        ).astype(jnp.bfloat16)


def rotate(rows_a, rows_b, b_out):
    return pl.pallas_call(
        rotate_kernel,
        out_shape=jax.ShapeDtypeStruct((512, INNER), jnp.bfloat16),
        in_specs=[pl.BlockSpec(memory_space=pltpu.VMEM)] * 3,
        out_specs=pl.BlockSpec(memory_space=pltpu.VMEM),
        compiler_params=pltpu.CompilerParams(vmem_limit_bytes=24 << 20),
        cost_estimate=pl.CostEstimate(
            flops=2 * 512 * INNER * INNER, bytes_accessed=5 << 20, transcendentals=0
        ),
    )(rows_a, rows_b, b_out)


def score_kernel(choice, home_ref, rows_a, rows_b, u_ref, qu_ref, q_acts, ids, before, *refs):
    n_pairs = len(choice)
    block_refs = refs[: sum(choice)]
    out_ref, held, sems = refs[sum(choice) :]
    home = home_ref[0] == 1

    def fetch(n, ref):
        return pltpu.make_async_copy(ref, held.at[n], sems.at[n])

    at = 0
    plan = []
    for n in range(n_pairs):
        plan.append(block_refs[at : at + choice[n]])
        at += choice[n]
        if choice[n] == 1:
            fetch(n, plan[n][0]).start()
        else:

            @pl.when(home)
            def _(n=n):
                fetch(n, plan[n][0]).start()

            @pl.when(jnp.logical_not(home))
            def _(n=n):
                fetch(n, plan[n][1]).start()

    norm_scale = 1.0 / math.sqrt(INNER * HIDDEN_SIZE)
    lanes = lax.broadcasted_iota(jnp.int32, (512, QUERIES), 1)
    total = before[...]
    for n in range(n_pairs):
        fetch(n, plan[n][0]).wait()
        basis = held[n, :HIDDEN_SIZE, :]
        weight = norm_scale / (held[n, HIDDEN_SIZE:, :].astype(jnp.float32) + DAMPING)
        query_v = jnp.dot(q_acts[...], basis, preferred_element_type=jnp.float32)
        train_v = jnp.concatenate(
            [
                jnp.dot(rows[:, :HIDDEN_SIZE], basis, preferred_element_type=jnp.float32)
                for rows in (rows_a, rows_b)
            ],
            axis=0,
        )
        train_v = train_v.astype(jnp.bfloat16).astype(jnp.float32)
        for q in range(QUERIES):
            chosen_v = jnp.where(ids[...] == q, query_v, 0.0).astype(jnp.bfloat16)
            rotated = jnp.dot(qu_ref[...], chosen_v, preferred_element_type=jnp.float32)
            precond = (rotated * weight).astype(jnp.bfloat16)
            project = jnp.dot(u_ref[...], precond, preferred_element_type=jnp.float32)
            score = jnp.sum(project * train_v, axis=1, keepdims=True)
            total = total + jnp.where(lanes == q, score, 0.0)
    out_ref[...] = total


def score(home, rows_a, rows_b, u, qu_t, q_acts, ids, before, blocks):
    choice = tuple(len(b) for b in blocks)
    flat = [x for b in blocks for x in b]
    width = flat[0].shape[1]
    n = len(blocks)
    vmem = pl.BlockSpec(memory_space=pltpu.VMEM)
    return pl.pallas_call(
        functools.partial(score_kernel, choice),
        out_shape=jax.ShapeDtypeStruct((512, QUERIES), jnp.float32),
        in_specs=[pl.BlockSpec(memory_space=pltpu.SMEM)]
        + [vmem] * 7
        + [pl.BlockSpec(memory_space=pl.ANY)] * len(flat),
        out_specs=vmem,
        scratch_shapes=[
            pltpu.VMEM((n, HIDDEN_SIZE + INNER, width), jnp.bfloat16),
            pltpu.SemaphoreType.DMA((n,)),
        ],
        compiler_params=pltpu.CompilerParams(vmem_limit_bytes=40 << 20),
        cost_estimate=pl.CostEstimate(
            flops=n * 2 * 512 * width * (HIDDEN_SIZE + QUERIES * INNER),
            bytes_accessed=(4 + 2 * n) << 20,
            transcendentals=0,
        ),
    )(home, rows_a, rows_b, u, qu_t, q_acts, ids, before, *flat)


def on_device(
    train_acts,
    train_grads,
    slot_counts,
    query_acts,
    query_grads,
    query_ids,
    basis_in,
    eigen_vals,
    basis_out,
):
    core, xl, y = lax.axis_index("core"), lax.axis_index("xl"), lax.axis_index("y")
    turn = y // 2
    is_home = core == xl
    home = is_home.astype(jnp.int32).reshape(1)
    groups = route_groups()

    def pick(array, which):
        return lax.dynamic_index_in_dim(array, which, 0, keepdims=False)[0]

    def weights(which):
        return jnp.concatenate([pick(basis_in, which), pick(eigen_vals, which)], axis=0)

    far, own = weights(1 - turn), weights(turn)
    first = send(far, outer_step, cross_step)
    second = send(own, inner_step, cross_step)

    train_acts, train_grads, _, _ = lax.optimization_barrier((train_acts, train_grads, far, own))
    rows = jnp.concatenate(
        [
            train_acts.reshape(64, SLOTS, HIDDEN_SIZE),
            train_grads.reshape(64, SLOTS, INNER),
        ],
        axis=2,
    )
    mine = lax.all_to_all(rows, AXES, 0, 0, axis_index_groups=groups, tiled=True)

    third = send(first, inner_step, outer_step)
    fourth = send(second, None, inner_step)
    fifth = send(third, None, inner_step)

    mine, third, fourth = lax.optimization_barrier((mine, third, fourth))
    mine = mine.reshape(256, HIDDEN_SIZE + INNER)
    theirs = other_core(mine)

    query_acts, query_grads, query_ids, basis_out, second = lax.optimization_barrier(
        (query_acts, query_grads, query_ids, basis_out, second)
    )

    def from_home(x):
        return jnp.where(is_home, x, other_core(x))

    q_acts = from_home(pick(query_acts, turn))
    q_grads = from_home(pick(query_grads, turn))
    q_ids = from_home(pick(query_ids, turn)).reshape(-1, 1)
    b_out = from_home(pick(basis_out, turn))
    qu_t = jnp.dot(q_grads, b_out, preferred_element_type=jnp.float32).astype(jnp.bfloat16).T

    u = rotate(mine, theirs, b_out)
    total = jnp.zeros((512, QUERIES), jnp.float32)
    for blocks in (((second,), (third,)), ((own, fourth),), ((first, fifth),)):
        total = score(home, mine, theirs, u, qu_t, q_acts, q_ids, total, blocks)
    mine_sum = total[:256] + other_core(total[256:])
    back = lax.all_to_all(
        mine_sum.reshape(64, SLOTS, QUERIES), AXES, 0, 0, axis_index_groups=groups, tiled=True
    )
    counts = slot_counts[0].reshape(64)
    live = jnp.arange(SLOTS)[None, :] < counts[:, None]
    return jnp.where(live[:, :, None], back, 0.0).reshape(256, QUERIES).T


def solution(mesh):
    grid = Mesh(mesh.devices.reshape(SIZES), AXES)
    expert, shard = ("xh", "z", "core"), ("xl", "y")
    whole = expert + shard
    in_specs = (
        P(whole, None),
        P(whole, None),
        P(whole, None, None),
        P(None, expert, None, None),
        P(None, expert, None, None),
        P(None, expert, None),
        P(None, expert, None, shard),
        P(None, expert, None, shard),
        P(None, expert, None, None),
    )
    return jax.shard_map(
        on_device, mesh=grid, in_specs=in_specs, out_specs=P(None, whole), check_vma=False
    )
```

profile of v0, /device:TPU:1, one launch (start us, length us, event | category | flops | bytes accessed | tf_op | source)
XLA Modules:
  0.0 128.7 jit_solution(9140883053727017740)
XLA Ops:
  0.0 1.8 %dynamic-slice_bitcast_fusion.1 = (bf16[2048,256]{1,0:T(8,128)(2,1)S(1)}, bf16[2048,256]{1,0:T(8,128)(2,1)S(1)}) fusion(bf16[2,1,2048,256]{3,2,1,0:T(8,128)(2,1)} %param.15, s32[]{:T(128)S(6)} %select_n.61, s32[]{:T(128)S(6)} %select_n.60), kind=kLoop, calls=%fused_computation.6 | loop fusion | bytes 4194312 | tf_op jit(solution)/shard_map/squeeze | solution.py:194
  2.0 2.7 %collective-permute-start.2 = (bf16[2816,256]{1,0:T(8,128)(2,1)S(1)}, bf16[2816,256]{1,0:T(8,128)(2,1)}, u32[]{:S(2)}, u32[]{:S(2)}) collective-permute-start(bf16[2816,256]{1,0:T(8,128)(2,1)S(1)} %pad_maximum_fusion.1.refs_0_), channel_id=1, source_target_pairs={{0,1},{1,0},{2,3},{3,2},{4,8},{5,9},{6,10},{7,11},{8,4},{9,5},{10,... | collective-permute-start | bytes 4325384 | tf_op jit(solution)/shard_map/ppermute | solution.py:71
  4.7 1.2 pad_maximum_fusion
  6.2 2.3 %reshape.57 = bf16[64,4,2048]{2,1,0:T(4,128)(2,1)} reshape(bf16[256,2048]{1,0:T(8,128)(2,1)} %param.9) | data formatting | bytes 2097152 | tf_op jit(solution)/shard_map/reshape | solution.py:206
  8.5 1.1 reshape.58
  9.6 3.1 %pad_maximum_fusion.2 = bf16[64,4,2816]{2,1,0:T(4,128)(2,1)} fusion(bf16[64,4,768]{2,1,0:T(4,128)(2,1)S(1)} %reshape.58, bf16[64,4,2048]{2,1,0:T(4,128)(2,1)} %reshape.57), kind=kLoop, calls=%fused_computation.2 | loop fusion | flops 2883584 | bytes 2883584 | tf_op jit(solution)/shard_map/concatenate | solution.py:204
  12.7 14.0 %all-to-all-start = ((bf16[64,4,2816]{2,1,0:T(4,128)(2,1)}), bf16[64,4,2816]{2,1,0:T(4,128)(2,1)}, u32[]{:S(2)}, u32[]{:S(2)}) async-start(bf16[64,4,2816]{2,1,0:T(4,128)(2,1)} %pad_maximum_fusion.2), calls=%async_computation | async-start | bytes 2883584 | tf_op jit(solution)/shard_map/all_to_all | solution.py:211
  26.8 1.9 %collective-permute-start.3 = (bf16[2816,256]{1,0:T(8,128)(2,1)}, bf16[2816,256]{1,0:T(8,128)(2,1)S(1)}, u32[]{:S(2)}, u32[]{:S(2)}) collective-permute-start(bf16[2816,256]{1,0:T(8,128)(2,1)} %collective-permute-done.2.refs_0_), channel_id=1, source_target_pairs={{4,5},{5,4},{6,7},{7,6},{8,9},{9,8},{10,11},{11,10},{20,21},{21,20... | collective-permute-start | bytes 4325384 | tf_op jit(solution)/shard_map/ppermute | solution.py:71
  28.7 15.1 %collective-permute-done.refs_0_ = bf16[2816,256]{1,0:T(8,128)(2,1)S(1)} collective-permute-done((bf16[2816,256]{1,0:T(8,128)(2,1)}, bf16[2816,256]{1,0:T(8,128)(2,1)S(1)}, u32[]{:S(2)}, u32[]{:S(2)}) %collective-permute-start) | collective-permute-done | bytes 1441824 | tf_op jit(solution)/shard_map/ppermute | solution.py:71
  43.8 2.9 %collective-permute-start.1 = (bf16[2816,256]{1,0:T(8,128)(2,1)S(1)}, bf16[2816,256]{1,0:T(8,128)(2,1)}, u32[]{:S(2)}, u32[]{:S(2)}) collective-permute-start(bf16[2816,256]{1,0:T(8,128)(2,1)S(1)} %collective-permute-done.refs_0_), channel_id=1, source_target_pairs={{0,1},{1,0},{2,3},{3,2},{4,7},{5,6},{6,5},{7,4},{8,11},{9,10},{10,... | collective-permute-start | bytes 4325384 | tf_op jit(solution)/shard_map/ppermute | solution.py:71
  46.6 2.4 %dynamic-slice_bitcast_fusion = bf16[768,768]{1,0:T(8,128)(2,1)} fusion(bf16[2,1,768,768]{3,2,1,0:T(8,128)(2,1)} %param.17, s32[]{:T(128)S(6)} %select_n.61), kind=kLoop, calls=%fused_computation.3 | loop fusion | bytes 2359300 | tf_op jit(solution)/shard_map/squeeze | solution.py:194
  49.0 1.0 dynamic-slice_bitcast_fusion.5
  50.0 0.6 collective-permute-start.7
  50.6 11.2 %all-to-all-done = bf16[64,4,2816]{2,1,0:T(4,128)(2,1)} async-done(((bf16[64,4,2816]{2,1,0:T(4,128)(2,1)}), bf16[64,4,2816]{2,1,0:T(4,128)(2,1)}, u32[]{:S(2)}, u32[]{:S(2)}) %all-to-all-start) | async-done | bytes 1441824 | tf_op jit(solution)/shard_map/all_to_all | solution.py:211
  61.8 0.6 collective-permute-done.3.refs_1_
  62.4 1.2 copy-done.5
  63.6 7.2 %collective-permute-done.1.refs_1_ = bf16[2816,256]{1,0:T(8,128)(2,1)} collective-permute-done((bf16[2816,256]{1,0:T(8,128)(2,1)S(1)}, bf16[2816,256]{1,0:T(8,128)(2,1)}, u32[]{:S(2)}, u32[]{:S(2)}) %collective-permute-start.1) | collective-permute-done | bytes 1441824 | tf_op jit(solution)/shard_map/ppermute | solution.py:71
  70.9 2.6 %reshape.59.rows_a = bf16[256,2816]{1,0:T(8,128)(2,1)S(1)} reshape(bf16[64,4,2816]{2,1,0:T(4,128)(2,1)} %all-to-all-done) | data formatting | bytes 2883584 | tf_op jit(solution)/shard_map/reshape | solution.py:218
  74.3 2.5 %collective-permute-done.8 = s32[64]{0:T(128)S(1)} collective-permute-done((s32[64]{0:T(128)S(1)}, s32[64]{0:T(128)S(1)}, u32[]{:S(2)}, u32[]{:S(2)}) %collective-permute-start.8) | collective-permute-done | bytes 288 | tf_op jit(solution)/shard_map/ppermute | solution.py:75
  76.9 2.1 %collective-permute-start.9 = (bf16[2816,256]{1,0:T(8,128)(2,1)}, bf16[2816,256]{1,0:T(8,128)(2,1)S(1)}, u32[]{:S(2)}, u32[]{:S(2)}) collective-permute-start(bf16[2816,256]{1,0:T(8,128)(2,1)} %collective-permute-done.1.refs_1_), channel_id=1, source_target_pairs={{4,5},{5,4},{6,7},{7,6},{8,9},{9,8},{10,11},{11,10},{20,21},{21,20... | collective-permute-start | bytes 4325384 | tf_op jit(solution)/shard_map/ppermute | solution.py:71
  79.0 1.1 broadcast_select_fusion.1.q_acts
  80.1 1.8 %broadcast_select_fusion.b_out = bf16[768,768]{1,0:T(8,128)(2,1)S(1)} fusion(bf16[768,768]{1,0:T(8,128)(2,1)} %collective-permute-done.5, pred[]{:T(512)S(6)} %eq.3, bf16[2,1,768,768]{3,2,1,0:T(8,128)(2,1)} %param.17, s32[]{:T(128)S(6)} %select_n.61), kind=kLoop, calls=%fused_computation.4 | loop fusion | flops 589824 | bytes 3538949 | tf_op jit(solution)/shard_map/jit(_where)/select_n | solution.py:226
  81.9 1.4 %convolution_convert_fusion.qu_ref = bf16[768,64]{1,0:T(8,128)(2,1)S(1)} fusion(bf16[768,768]{1,0:T(8,128)(2,1)S(1)} %broadcast_select_fusion.b_out, bf16[64,768]{1,0:T(8,128)(2,1)S(1)} %dynamic-slice_bitcast_fusion.6, bf16[64,768]{1,0:T(8,128)(2,1)} %collective-permute-done.6, pred[]{:T(512)S(6)} %eq.3), kind=kOutput, calls=%fused_computation.5 | convolution fusion | flops 75595776 | bytes 1474561 | tf_op jit(solution)/shard_map/dot_general | solution.py:232
  83.3 0.8 shard_map.91.u_ref
  84.1 8.9 %shard_map.92.before = f32[512,8]{1,0:T(8,128)S(1)} custom-call(s32[1]{0:T(128)} %bitcast.home_ref, bf16[256,2816]{1,0:T(8,128)(2,1)S(1)} %reshape.59.rows_a, bf16[256,2816]{1,0:T(8,128)(2,1)S(1)} %collective-permute-done.4.rows_b, bf16[512,768]{1,0:T(8,128)(2,1)S(1)} %shard_map.91.u_ref, bf16[768,64]{1,0:T(8,128)(2,1)S(1)} %convolution_convert_fusion.qu_ref, ...), custom_call_target="tpu_custom_call" | custom-call | flops 4294967296 | bytes 8388608 | tf_op jit(solution)/shard_map/pallas_call | solution.py:156
  93.1 4.0 %shard_map.93.before = f32[512,8]{1,0:T(8,128)S(1)} custom-call(s32[1]{0:T(128)} %bitcast.home_ref, bf16[256,2816]{1,0:T(8,128)(2,1)S(1)} %reshape.59.rows_a, bf16[256,2816]{1,0:T(8,128)(2,1)S(1)} %collective-permute-done.4.rows_b, bf16[512,768]{1,0:T(8,128)(2,1)S(1)} %shard_map.91.u_ref, bf16[768,64]{1,0:T(8,128)(2,1)S(1)} %convolution_convert_fusion.qu_ref, ...), custom_call_target="tpu_custom_call" | custom-call | flops 2147483648 | bytes 6291456 | tf_op jit(solution)/shard_map/pallas_call | solution.py:156
  97.1 4.3 %shard_map.94 = f32[512,8]{1,0:T(8,128)S(1)} custom-call(s32[1]{0:T(128)} %bitcast.home_ref, bf16[256,2816]{1,0:T(8,128)(2,1)S(1)} %reshape.59.rows_a, bf16[256,2816]{1,0:T(8,128)(2,1)S(1)} %collective-permute-done.4.rows_b, bf16[512,768]{1,0:T(8,128)(2,1)S(1)} %shard_map.91.u_ref, bf16[768,64]{1,0:T(8,128)(2,1)S(1)} %convolution_convert_fusion.qu_ref, ...), custom_call_target="tpu_custom_call" | custom-call | flops 2147483648 | bytes 6291456 | tf_op jit(solution)/shard_map/pallas_call | solution.py:156
  101.6 1.2 collective-permute-done.10
  102.9 0.7 slice_add_fusion
  103.5 13.8 %all-to-all-start.1 = ((f32[64,4,8]{2,1,0:T(4,128)}), f32[64,4,8]{2,1,0:T(4,128)S(1)}, u32[]{:S(2)}, u32[]{:S(2)}) async-start(f32[64,4,8]{2,1,0:T(4,128)} %bitcast.10), calls=%async_computation.1 | async-start | bytes 262144 | tf_op jit(solution)/shard_map/all_to_all | solution.py:239
  117.4 10.5 %all-to-all-done.1 = f32[64,4,8]{2,1,0:T(4,128)S(1)} async-done(((f32[64,4,8]{2,1,0:T(4,128)}), f32[64,4,8]{2,1,0:T(4,128)S(1)}, u32[]{:S(2)}, u32[]{:S(2)}) %all-to-all-start.1) | async-done | bytes 8224 | tf_op jit(solution)/shard_map/all_to_all | solution.py:239
  128.0 0.7 copy.19
  (42 shorter events, 1.9 us)
Async XLA Ops:
  0.0 74.1 %copy-start = (bf16[2,1,64,768]{3,2,1,0:T(8,128)(2,1)S(1)}, bf16[2,1,64,768]{3,2,1,0:T(8,128)(2,1)}, u32[]{:S(2)}) copy-start(bf16[2,1,64,768]{3,2,1,0:T(8,128)(2,1)} %param.13) | copy-start | bytes 589828
  0.0 1.8 %copy-start.7 = (bf16[2,1,768,256]{3,2,1,0:T(8,128)(2,1)S(1)}, bf16[2,1,768,256]{3,2,1,0:T(8,128)(2,1)}, u32[]{:S(2)}) copy-start(bf16[2,1,768,256]{3,2,1,0:T(8,128)(2,1)} %param.16) | copy-start | bytes 2359300
  2.0 3.9 %copy-start.1 = (bf16[2816,256]{1,0:T(8,128)(2,1)}, bf16[2816,256]{1,0:T(8,128)(2,1)S(1)}, u32[]{:S(2)}) copy-start(bf16[2816,256]{1,0:T(8,128)(2,1)S(1)} %pad_maximum_fusion.1.refs_0_) | copy-start | bytes 4325380
  2.0 24.8 %collective-permute-start.2 = (bf16[2816,256]{1,0:T(8,128)(2,1)S(1)}, bf16[2816,256]{1,0:T(8,128)(2,1)}, u32[]{:S(2)}, u32[]{:S(2)}) collective-permute-start(bf16[2816,256]{1,0:T(8,128)(2,1)S(1)} %pad_maximum_fusion.1.refs_0_), channel_id=1, source_target_pairs={{0,1},{1,0},{2,3},{3,2},{4,8},{5,9},{6,10},{7,11},{8,4},{9,5},{10,... | collective-permute-start | bytes 4325384 | tf_op jit(solution)/shard_map/ppermute | solution.py:71
  5.9 37.9 %collective-permute-start = (bf16[2816,256]{1,0:T(8,128)(2,1)}, bf16[2816,256]{1,0:T(8,128)(2,1)S(1)}, u32[]{:S(2)}, u32[]{:S(2)}) collective-permute-start(bf16[2816,256]{1,0:T(8,128)(2,1)} %pad_maximum_fusion), channel_id=1, source_target_pairs={{0,3},{1,2},{2,1},{3,0},{4,8},{5,9},{6,10},{7,11},{8,4},{9,5},{10,... | collective-permute-start | bytes 4325384 | tf_op jit(solution)/shard_map/ppermute | solution.py:71
  12.7 49.1 %all-to-all-start = ((bf16[64,4,2816]{2,1,0:T(4,128)(2,1)}), bf16[64,4,2816]{2,1,0:T(4,128)(2,1)}, u32[]{:S(2)}, u32[]{:S(2)}) async-start(bf16[64,4,2816]{2,1,0:T(4,128)(2,1)} %pad_maximum_fusion.2), calls=%async_computation | async-start | bytes 2883584 | tf_op jit(solution)/shard_map/all_to_all | solution.py:211
  26.8 35.6 %collective-permute-start.3 = (bf16[2816,256]{1,0:T(8,128)(2,1)}, bf16[2816,256]{1,0:T(8,128)(2,1)S(1)}, u32[]{:S(2)}, u32[]{:S(2)}) collective-permute-start(bf16[2816,256]{1,0:T(8,128)(2,1)} %collective-permute-done.2.refs_0_), channel_id=1, source_target_pairs={{4,5},{5,4},{6,7},{7,6},{8,9},{9,8},{10,11},{11,10},{20,21},{21,20... | collective-permute-start | bytes 4325384 | tf_op jit(solution)/shard_map/ppermute | solution.py:71
  43.8 6.2 %copy-start.3 = (bf16[2816,256]{1,0:T(8,128)(2,1)}, bf16[2816,256]{1,0:T(8,128)(2,1)S(1)}, u32[]{:S(2)}) copy-start(bf16[2816,256]{1,0:T(8,128)(2,1)S(1)} %collective-permute-done.refs_0_) | copy-start | bytes 4325380
  43.8 27.1 %collective-permute-start.1 = (bf16[2816,256]{1,0:T(8,128)(2,1)S(1)}, bf16[2816,256]{1,0:T(8,128)(2,1)}, u32[]{:S(2)}, u32[]{:S(2)}) collective-permute-start(bf16[2816,256]{1,0:T(8,128)(2,1)S(1)} %collective-permute-done.refs_0_), channel_id=1, source_target_pairs={{0,1},{1,0},{2,3},{3,2},{4,7},{5,6},{6,5},{7,4},{8,11},{9,10},{10,... | collective-permute-start | bytes 4325384 | tf_op jit(solution)/shard_map/ppermute | solution.py:71
  49.0 31.1 %collective-permute-start.5 = (bf16[768,768]{1,0:T(8,128)(2,1)}, bf16[768,768]{1,0:T(8,128)(2,1)}, u32[]{:S(2)}, u32[]{:S(2)}) collective-permute-start(bf16[768,768]{1,0:T(8,128)(2,1)} %dynamic-slice_bitcast_fusion), channel_id=1, source_target_pairs={{0,8},{8,0},{1,9},{9,1},{2,10},{10,2},{3,11},{11,3},{4,12},{12,4},... | collective-permute-start | bytes 3538952 | tf_op jit(solution)/shard_map/ppermute | solution.py:75
  50.0 23.6 %copy-start.8 = (s32[2,1,64]{2,1,0:T(1,128)S(1)}, s32[2,1,64]{2,1,0:T(1,128)}, u32[]{:S(2)}) copy-start(s32[2,1,64]{2,1,0:T(1,128)} %param.14) | copy-start | bytes 1540
  50.0 29.0 %collective-permute-start.7 = (bf16[64,2048]{1,0:T(8,128)(2,1)S(1)}, bf16[64,2048]{1,0:T(8,128)(2,1)}, u32[]{:S(2)}, u32[]{:S(2)}) collective-permute-start(bf16[64,2048]{1,0:T(8,128)(2,1)S(1)} %dynamic-slice_bitcast_fusion.5), channel_id=1, source_target_pairs={{0,8},{8,0},{1,9},{9,1},{2,10},{10,2},{3,11},{11,3},{4,12},{12,4},... | collective-permute-start | bytes 786440 | tf_op jit(solution)/shard_map/ppermute | solution.py:75
  62.4 1.2 copy-start.5
  73.5 9.8 %collective-permute-start.4 = (bf16[256,2816]{1,0:T(8,128)(2,1)S(1)}, bf16[256,2816]{1,0:T(8,128)(2,1)S(1)}, u32[]{:S(2)}, u32[]{:S(2)}) collective-permute-start(bf16[256,2816]{1,0:T(8,128)(2,1)S(1)} %reshape.59.rows_a), channel_id=1, source_target_pairs={{0,8},{8,0},{1,9},{9,1},{2,10},{10,2},{3,11},{11,3},{4,12},{12,4},... | collective-permute-start | bytes 4325384 | tf_op jit(solution)/shard_map/ppermute | solution.py:75
  73.6 3.2 %collective-permute-start.8 = (s32[64]{0:T(128)S(1)}, s32[64]{0:T(128)S(1)}, u32[]{:S(2)}, u32[]{:S(2)}) collective-permute-start(s32[64]{0:T(128)S(1)} %fusion.3), channel_id=1, source_target_pairs={{0,8},{8,0},{1,9},{9,1},{2,10},{10,2},{3,11},{11,3},{4,12},{12,4},... | collective-permute-start | bytes 776 | tf_op jit(solution)/shard_map/ppermute | solution.py:75
  74.1 7.8 %collective-permute-start.6 = (bf16[64,768]{1,0:T(8,128)(2,1)S(1)}, bf16[64,768]{1,0:T(8,128)(2,1)}, u32[]{:S(2)}, u32[]{:S(2)}) collective-permute-start(bf16[64,768]{1,0:T(8,128)(2,1)S(1)} %dynamic-slice_bitcast_fusion.6), channel_id=1, source_target_pairs={{0,8},{8,0},{1,9},{9,1},{2,10},{10,2},{3,11},{11,3},{4,12},{12,4},... | collective-permute-start | bytes 294920 | tf_op jit(solution)/shard_map/ppermute | solution.py:75
  76.9 20.2 %collective-permute-start.9 = (bf16[2816,256]{1,0:T(8,128)(2,1)}, bf16[2816,256]{1,0:T(8,128)(2,1)S(1)}, u32[]{:S(2)}, u32[]{:S(2)}) collective-permute-start(bf16[2816,256]{1,0:T(8,128)(2,1)} %collective-permute-done.1.refs_1_), channel_id=1, source_target_pairs={{4,5},{5,4},{6,7},{7,6},{8,9},{9,8},{10,11},{11,10},{20,21},{21,20... | collective-permute-start | bytes 4325384 | tf_op jit(solution)/shard_map/ppermute | solution.py:71
  84.1 8.9 %copy-start.2 = (bf16[2816,256]{1,0:T(8,128)(2,1)S(1)}, bf16[2816,256]{1,0:T(8,128)(2,1)}, u32[]{:S(2)}) copy-start(bf16[2816,256]{1,0:T(8,128)(2,1)} %copy-done.1) | copy-start | bytes 4325380
  84.1 8.9 %copy-start.6 = (bf16[2816,256]{1,0:T(8,128)(2,1)S(1)}, bf16[2816,256]{1,0:T(8,128)(2,1)}, u32[]{:S(2)}) copy-start(bf16[2816,256]{1,0:T(8,128)(2,1)} %copy-done.5) | copy-start | bytes 4325380
  93.1 4.1 %copy-start.4 = (bf16[2816,256]{1,0:T(8,128)(2,1)S(1)}, bf16[2816,256]{1,0:T(8,128)(2,1)}, u32[]{:S(2)}) copy-start(bf16[2816,256]{1,0:T(8,128)(2,1)} %copy-done.3) | copy-start | bytes 4325380
  97.1 4.4 %copy-start.9 = (s32[1,2,32]{2,1,0:T(2,128)S(1)}, s32[1,2,32]{2,1,0:T(2,128)}, u32[]{:S(2)}) copy-start(s32[1,2,32]{2,1,0:T(2,128)} %param.11) | copy-start | bytes 772
  101.4 1.4 %collective-permute-start.10 = (f32[256,8]{1,0:T(8,128)S(1)}, f32[256,8]{1,0:T(8,128)S(1)}, u32[]{:S(2)}, u32[]{:S(2)}) collective-permute-start(f32[256,8]{1,0:T(8,128)S(1)} %slice.9), channel_id=1, source_target_pairs={{0,8},{8,0},{1,9},{9,1},{2,10},{10,2},{3,11},{11,3},{4,12},{12,4},... | collective-permute-start | bytes 24584 | tf_op jit(solution)/shard_map/ppermute | solution.py:75
  103.5 24.4 %all-to-all-start.1 = ((f32[64,4,8]{2,1,0:T(4,128)}), f32[64,4,8]{2,1,0:T(4,128)S(1)}, u32[]{:S(2)}, u32[]{:S(2)}) async-start(f32[64,4,8]{2,1,0:T(4,128)} %bitcast.10), calls=%async_computation.1 | async-start | bytes 262144 | tf_op jit(solution)/shard_map/all_to_all | solution.py:239
where the time goes:
time: 129 us
  waiting for transfers between devices  48.3 us (37%)
  starting transfers between devices  39.2 us (30%)
  Pallas kernels  18 us (14%)
  local copies, waits for them, and re-layouts  13.3 us (10%)
  other arithmetic  8.13 us (6%)
  matrix products  1.42 us (1%)
    ppermute x5, waiting for transfers between devices, send(): return lax.ppermute(x, ('core', 'xl', 'y'), moves(home_step, guest_step))  22.9 us
    pallas_call x3, Pallas kernels, score(): pl.pallas_call(functools.partial(score_kernel, choice), out_shape=jax.Sha...  17.2 us
    all_to_all x1, starting transfers between devices, on_device(): lax.all_to_all(rows, AXES, 0, 0, axis_index_groups=groups, tiled=True)  14 us
    all_to_all x1, starting transfers between devices, on_device(): lax.all_to_all(mine_sum.reshape(64, SLOTS, QUERIES), AXES, 0, 0, axis_ind...  13.8 us
    all_to_all x1, waiting for transfers between devices, on_device(): lax.all_to_all(rows, AXES, 0, 0, axis_index_groups=groups, tiled=True)  11.2 us
    all_to_all x1, waiting for transfers between devices, on_device(): lax.all_to_all(mine_sum.reshape(64, SLOTS, QUERIES), AXES, 0, 0, axis_ind...  10.5 us
    ppermute x5, starting transfers between devices, send(): return lax.ppermute(x, ('core', 'xl', 'y'), moves(home_step, guest_step))  9.9 us
    squeeze x6, local copies, waits for them, and re-layouts, pick(): return lax.dynamic_index_in_dim(array, which, 0, keepdims=False)[0]  5.17 us
  transfers between devices with their start and end apart: 13, of which 7 were waited for; matrix products, arithmetic and copies ran while one was open for 14% of the time, Pallas kernels for 11%

commit v1 on v0

v1 whole, which is shorter than its diff:
```python
import functools
import math

import jax
import jax.numpy as jnp
from jax import lax
from jax.experimental import pallas as pl
from jax.experimental.pallas import tpu as pltpu
from jax.sharding import Mesh, PartitionSpec as P

HIDDEN_SIZE = 2048
INNER = 768
QUERIES = 8
SLOTS = 4
TURNS = 2
DAMPING = 0.05

SIZES = (2, 8, 2, 2, 4)
AXES = ("xh", "z", "core", "xl", "y")


def flat_index(xh, z, core, xl, y):
    return (((xh * 8 + z) * 2 + core) * 2 + xl) * 4 + y


def route_groups():
    groups = []
    for core in range(2):
        for low in range(2):
            turn_y = (low, 3 - low)
            groups.append(
                [
                    flat_index(xh, z, core, xl, turn_y[k])
                    for k in range(2)
                    for xh in range(2)
                    for z in range(8)
                    for xl in range(2)
                ]
            )
    return groups


def moves(home_step, guest_step):
    pairs = []
    for core in range(2):
        for xl in range(2):
            for y in range(4):
                step = home_step if core == xl else guest_step
                if step is not None:
                    pairs.append(((core * 2 + xl) * 4 + y, step(core, xl, y)))
    return pairs


def place(core, xl, y):
    return (core * 2 + xl) * 4 + y


def cross_step(core, xl, y):
    return place(1 - core, 1 - xl, y)


def outer_step(core, xl, y):
    return place(core, xl, 3 - y)


def inner_step(core, xl, y):
    return place(core, xl, y ^ 1)


def send(x, home_step, guest_step):
    return lax.ppermute(x, ("core", "xl", "y"), moves(home_step, guest_step))


def other_core(x):
    return lax.ppermute(x, "core", [(0, 1), (1, 0)])


def load(pairs, sems):
    copies = [
        pltpu.make_async_copy(src, dst, sems.at[n]) for n, (src, dst) in enumerate(pairs)
    ]
    for each in copies:
        each.start()
    for each in copies:
        each.wait()


def through(chunks, sems):
    inward = [
        pltpu.make_async_copy(src, mid, sems.at[0, n]) for n, (src, mid, _) in enumerate(chunks)
    ]
    outward = [
        pltpu.make_async_copy(mid, dst, sems.at[1, n]) for n, (_, mid, dst) in enumerate(chunks)
    ]
    for each in inward:
        each.start()
    for before, after in zip(inward, outward):
        before.wait()
        after.start()
    for each in outward:
        each.wait()


def block_kernel(which_ref, basis, eigen, after, block, held, sems):
    which = which_ref[0]
    chunks = []
    for start in range(0, HIDDEN_SIZE, 512):
        span = pl.ds(start, 512)
        chunks.append((basis.at[which, 0, span], held.at[span], block.at[span]))
    span = pl.ds(HIDDEN_SIZE, INNER)
    chunks.append((eigen.at[which, 0], held.at[span], block.at[span]))
    through(chunks, sems)


def query_pack_kernel(
    turn_ref, ids, q_acts, q_grads, b_out, after, q_pack, b_pack, q_held, b_held, sems
):
    turn = turn_ref[0]
    id_row = jnp.where(turn == 0, ids[0], ids[1]).astype(jnp.float32)
    b_held[INNER + 64 :, :] = jnp.zeros((16, INNER), jnp.bfloat16)
    b_held[INNER + 64 :, :64] = jnp.broadcast_to(id_row, (16, 64)).astype(jnp.bfloat16)
    load(
        [
            (q_acts.at[turn, 0], q_held),
            (b_out.at[turn, 0], b_held.at[pl.ds(0, INNER)]),
            (q_grads.at[turn, 0], b_held.at[pl.ds(INNER, 64)]),
        ],
        sems,
    )
    load([(q_held, q_pack), (b_held, b_pack)], sems)


def rows_kernel(acts, grads, after, rows):
    rows[:, :, :HIDDEN_SIZE] = acts[...].reshape(64, SLOTS, HIDDEN_SIZE)
    rows[:, :, HIDDEN_SIZE:] = grads[...].reshape(64, SLOTS, INNER)


VMEM = pl.BlockSpec(memory_space=pltpu.VMEM)
HBM = pl.BlockSpec(memory_space=pltpu.HBM)
ANY = pl.BlockSpec(memory_space=pl.ANY)
SMEM = pl.BlockSpec(memory_space=pltpu.SMEM)
BLOCK = jax.ShapeDtypeStruct((HIDDEN_SIZE + INNER, 256), jnp.bfloat16)


def pack_block(which, basis, eigen, after):
    return pl.pallas_call(
        block_kernel,
        out_shape=BLOCK,
        in_specs=[SMEM, HBM, HBM, ANY],
        out_specs=HBM,
        scratch_shapes=[pltpu.VMEM(BLOCK.shape, BLOCK.dtype), pltpu.SemaphoreType.DMA((2, 5))],
        compiler_params=pltpu.CompilerParams(vmem_limit_bytes=60 << 20),
    )(which, basis, eigen, after)


def pack_query(turn, ids, q_acts, q_grads, b_out, after):
    return pl.pallas_call(
        query_pack_kernel,
        out_shape=[
            jax.ShapeDtypeStruct((64, HIDDEN_SIZE), jnp.bfloat16),
            jax.ShapeDtypeStruct((INNER + 80, INNER), jnp.bfloat16),
        ],
        in_specs=[SMEM, VMEM] + [HBM] * 3 + [ANY],
        out_specs=[ANY] * 2,
        scratch_shapes=[
            pltpu.VMEM((64, HIDDEN_SIZE), jnp.bfloat16),
            pltpu.VMEM((INNER + 80, INNER), jnp.bfloat16),
            pltpu.SemaphoreType.DMA((3,)),
        ],
        compiler_params=pltpu.CompilerParams(vmem_limit_bytes=60 << 20),
    )(turn, ids, q_acts, q_grads, b_out, after)


def pack_rows(acts, grads, after):
    return pl.pallas_call(
        rows_kernel,
        out_shape=jax.ShapeDtypeStruct((64, SLOTS, HIDDEN_SIZE + INNER), jnp.bfloat16),
        in_specs=[VMEM, VMEM, ANY],
        out_specs=VMEM,
        compiler_params=pltpu.CompilerParams(vmem_limit_bytes=60 << 20),
    )(acts, grads, after)


def query_kernel(
    home_ref, q_own, q_other, b_own, b_other, q_acts, b_out, qu_ref, ids_ref, b_pack, sems
):
    home = home_ref[0] == 1
    options = [((b, b_pack), (q, q_acts)) for q, b in ((q_own, b_own), (q_other, b_other))]
    each_option(home, options, lambda pairs: load(pairs, sems))
    b_out[...] = b_pack[:INNER, :]
    rotated = jnp.dot(
        b_pack[INNER : INNER + 64, :], b_out[...], preferred_element_type=jnp.float32
    )
    turned = jnp.concatenate([rotated, jnp.zeros_like(rotated)], axis=0).T
    qu_ref[...] = turned[:, :64].astype(jnp.bfloat16)
    ids = b_pack[INNER + 64 : INNER + 80, :].astype(jnp.float32)[:1, :128]
    ids_ref[...] = jnp.broadcast_to(ids, (128, 128)).T[:64, :]


def query(home, q_own, q_other, b_own, b_other):
    bf16 = jnp.bfloat16
    return pl.pallas_call(
        query_kernel,
        out_shape=[
            jax.ShapeDtypeStruct((64, HIDDEN_SIZE), bf16),
            jax.ShapeDtypeStruct((INNER, INNER), bf16),
            jax.ShapeDtypeStruct((INNER, 64), bf16),
            jax.ShapeDtypeStruct((64, 128), jnp.float32),
        ],
        in_specs=[SMEM] + [ANY] * 4,
        out_specs=[VMEM] * 4,
        scratch_shapes=[
            pltpu.VMEM((INNER + 80, INNER), bf16),
            pltpu.SemaphoreType.DMA((2,)),
        ],
        compiler_params=pltpu.CompilerParams(vmem_limit_bytes=24 << 20),
        cost_estimate=pl.CostEstimate(
            flops=2 * 64 * INNER * INNER, bytes_accessed=5 << 20, transcendentals=0
        ),
    )(home, q_own, q_other, b_own, b_other)


def each_option(home, options, act):
    if len(options) == 1:
        act(options[0])
    else:
        pl.when(home)(lambda: act(options[0]))
        pl.when(jnp.logical_not(home))(lambda: act(options[1]))


def fetch_blocks(home, choice, refs, held, sems):
    plan, at = [], 0
    for n, count in enumerate(choice):
        plan.append(
            [pltpu.make_async_copy(ref, held.at[n], sems.at[n]) for ref in refs[at : at + count]]
        )
        each_option(home, plan[n], lambda copy: copy.start())
        at += count
    return plan


def block_weight(held, n):
    norm_scale = 1.0 / math.sqrt(INNER * HIDDEN_SIZE)
    return norm_scale / (held[n, HIDDEN_SIZE:, :].astype(jnp.float32) + DAMPING)


def rotate_acts(acts, basis):
    train_v = jnp.dot(acts, basis, preferred_element_type=jnp.float32)
    return train_v.astype(jnp.bfloat16).astype(jnp.float32)


def precondition(qu_ref, ids_ref, query_v, weight, q):
    chosen_v = jnp.where(ids_ref[:, :1] == q, query_v, 0.0).astype(jnp.bfloat16)
    rotated = jnp.dot(qu_ref[...], chosen_v, preferred_element_type=jnp.float32)
    return (rotated * weight).astype(jnp.bfloat16)


def add_score(total, q, u, precond, train_v):
    lanes = lax.broadcasted_iota(jnp.int32, total.shape, 1)
    project = jnp.dot(u, precond, preferred_element_type=jnp.float32)
    score = jnp.sum(project * train_v, axis=1, keepdims=True)
    return total + jnp.where(lanes == q, score, 0.0)


def add_blocks(home, plan, held, acts, u_ref, qu_ref, ids_ref, q_acts, total, kept=None):
    for n, options in enumerate(plan):
        each_option(home, options, lambda copy: copy.wait())
        basis = held[n, :HIDDEN_SIZE, :]
        weight = block_weight(held, n)
        query_v = jnp.dot(q_acts[...], basis, preferred_element_type=jnp.float32)
        train_v = rotate_acts(acts[...], basis)
        for q in range(QUERIES):
            precond = precondition(qu_ref, ids_ref, query_v, weight, q)
            if kept is not None:
                kept[n, pl.ds(q * INNER, INNER), :] = precond
            total = add_score(total, q, u_ref[...], precond, train_v)
    return total


def unpack_rows(rows, b_out, acts, u_ref):
    acts[...] = rows[:, :, :HIDDEN_SIZE].reshape(256, HIDDEN_SIZE)
    u_ref[...] = jnp.dot(
        rows[:, :, HIDDEN_SIZE:].reshape(256, INNER),
        b_out[...],
        preferred_element_type=jnp.float32,
    ).astype(jnp.bfloat16)


def early_kernel(choice, home_ref, rows, b_out, qu_ref, ids_ref, q_acts, *refs):
    count = sum(choice)
    mine_ref, acts, u_ref, kept, held, sems = refs[count:]
    home = home_ref[0] == 1
    plan = fetch_blocks(home, choice, refs[:count], held, sems)
    unpack_rows(rows, b_out, acts, u_ref)
    total = jnp.zeros((256, QUERIES), jnp.float32)
    mine_ref[...] = add_blocks(
        home, plan, held, acts, u_ref, qu_ref, ids_ref, q_acts, total, kept
    )


def late_kernel(acts, u_ref, kept, *refs):
    n_blocks = kept.shape[0]
    sent_ref, held, sems = refs[n_blocks:]
    copies = [
        pltpu.make_async_copy(ref.at[pl.ds(0, HIDDEN_SIZE)], held.at[n], sems.at[n])
        for n, ref in enumerate(refs[:n_blocks])
    ]
    for each in copies:
        each.start()
    total = jnp.zeros((256, QUERIES), jnp.float32)
    for n, each in enumerate(copies):
        each.wait()
        train_v = rotate_acts(acts[...], held[n])
        for q in range(QUERIES):
            total = add_score(
                total, q, u_ref[...], kept[n, pl.ds(q * INNER, INNER), :], train_v
            )
    sent_ref[...] = total


def score_kernel(
    choice, home_ref, acts_a, u_a, acts_b, u_b, qu_ref, ids_ref, q_acts, mine_in, sent_in, *refs
):
    count = sum(choice)
    mine_ref, sent_ref, held, acts, u_ref, sems = refs[count:]
    home = home_ref[0] == 1
    plan = fetch_blocks(home, choice, refs[:count], held, sems)
    acts[:256], acts[256:] = acts_a[...], acts_b[...]
    u_ref[:256], u_ref[256:] = u_a[...], u_b[...]
    total = jnp.concatenate([mine_in[...], sent_in[...]], axis=0)
    total = add_blocks(home, plan, held, acts, u_ref, qu_ref, ids_ref, q_acts, total)
    mine_ref[...] = total[:256]
    sent_ref[...] = total[256:]


HALF = jax.ShapeDtypeStruct((256, QUERIES), jnp.float32)


def score_cost(n):
    return pl.CostEstimate(flops=n, bytes_accessed=n, transcendentals=0)


ACTS = jax.ShapeDtypeStruct((256, HIDDEN_SIZE), jnp.bfloat16)
GRADS = jax.ShapeDtypeStruct((256, INNER), jnp.bfloat16)


def score_early(home, rows, b_out, queries, blocks):
    choice = tuple(len(options) for options in blocks)
    flat = [x for options in blocks for (x,) in options]
    n = len(blocks)
    return pl.pallas_call(
        functools.partial(early_kernel, choice),
        out_shape=[
            HALF,
            ACTS,
            GRADS,
            jax.ShapeDtypeStruct((n, QUERIES * INNER, 256), jnp.bfloat16),
        ],
        in_specs=[SMEM] + [VMEM] * 5 + [ANY] * len(flat),
        out_specs=[VMEM] * 4,
        scratch_shapes=[
            pltpu.VMEM((n, HIDDEN_SIZE + INNER, 256), jnp.bfloat16),
            pltpu.SemaphoreType.DMA((n,)),
        ],
        compiler_params=pltpu.CompilerParams(vmem_limit_bytes=28 << 20),
        cost_estimate=score_cost(n),
    )(home, rows, b_out, *queries, *flat)


def score_late(acts, u, kept, blocks):
    n = len(blocks)
    return pl.pallas_call(
        late_kernel,
        out_shape=HALF,
        in_specs=[VMEM] * 3 + [ANY] * n,
        out_specs=VMEM,
        scratch_shapes=[
            pltpu.VMEM((n, HIDDEN_SIZE, 256), jnp.bfloat16),
            pltpu.SemaphoreType.DMA((n,)),
        ],
        compiler_params=pltpu.CompilerParams(vmem_limit_bytes=24 << 20),
        cost_estimate=score_cost(n),
    )(acts, u, kept, *blocks)


def score(home, rows, queries, mine_sum, sent, blocks):
    choice = tuple(len(options) for options in blocks)
    flat = [x for options in blocks for (x,) in options]
    n = len(blocks)
    return pl.pallas_call(
        functools.partial(score_kernel, choice),
        out_shape=[HALF, HALF],
        in_specs=[SMEM] + [VMEM] * 9 + [ANY] * len(flat),
        out_specs=[VMEM] * 2,
        scratch_shapes=[
            pltpu.VMEM((n, HIDDEN_SIZE + INNER, 256), jnp.bfloat16),
            pltpu.VMEM((512, HIDDEN_SIZE), jnp.bfloat16),
            pltpu.VMEM((512, INNER), jnp.bfloat16),
            pltpu.SemaphoreType.DMA((n,)),
        ],
        compiler_params=pltpu.CompilerParams(vmem_limit_bytes=24 << 20),
        cost_estimate=score_cost(n),
    )(home, *rows, *queries, mine_sum, sent, *flat)


def on_device(
    train_acts,
    train_grads,
    slot_counts,
    query_acts,
    query_grads,
    query_ids,
    basis_in,
    eigen_vals,
    basis_out,
):
    core, xl, y = lax.axis_index("core"), lax.axis_index("xl"), lax.axis_index("y")
    turn = y // 2
    is_home = core == xl
    home = is_home.astype(jnp.int32).reshape(1)
    groups = route_groups()

    turn_ref = turn.astype(jnp.int32).reshape(1)
    far = pack_block(1 - turn_ref, basis_in, eigen_vals, turn_ref)
    first = send(far, outer_step, cross_step)
    token = other_core(far[:8])
    own = pack_block(turn_ref, basis_in, eigen_vals, token)
    second = send(own, inner_step, cross_step)
    rows = pack_rows(train_acts, train_grads, far)
    rows, own = lax.optimization_barrier((rows, own))
    mine = lax.all_to_all(rows, AXES, 0, 0, axis_index_groups=groups, tiled=True)
    third = send(first, inner_step, outer_step)
    fifth = send(third, None, inner_step)
    q_own, b_own = pack_query(turn_ref, query_ids, query_acts, query_grads, basis_out, first)
    q_acts, b_out, qu, ids = query(home, q_own, other_core(q_own), b_own, other_core(b_own))
    held_second, qu = lax.optimization_barrier((second, qu))
    fourth = send(held_second, None, inner_step)
    queries = (qu, ids, q_acts)
    mine_sum, acts_a, u_a, kept = score_early(
        home, mine, b_out, queries, [[(second,)], [(third,)]]
    )
    acts_a, u_a, fourth = lax.optimization_barrier((acts_a, u_a, fourth))
    acts_b, u_b = other_core(acts_a), other_core(u_a)
    sent = score_late(acts_b, u_b, kept, [second, third])
    rows = (acts_a, u_a, acts_b, u_b)
    for blocks in ([[(own,), (fourth,)]], [[(first,), (fifth,)]]):
        mine_sum, sent = score(home, rows, queries, mine_sum, sent, blocks)
    mine_sum = mine_sum + other_core(sent)
    back = lax.all_to_all(
        mine_sum.reshape(64, SLOTS, QUERIES), AXES, 0, 0, axis_index_groups=groups, tiled=True
    )
    counts = slot_counts[0].reshape(64)
    live = jnp.arange(SLOTS)[None, :] < counts[:, None]
    return jnp.where(live[:, :, None], back, 0.0).reshape(256, QUERIES).T


def solution(mesh):
    grid = Mesh(mesh.devices.reshape(SIZES), AXES)
    expert, shard = ("xh", "z", "core"), ("xl", "y")
    whole = expert + shard
    in_specs = (
        P(whole, None),
        P(whole, None),
        P(whole, None, None),
        P(None, expert, None, None),
        P(None, expert, None, None),
        P(None, expert, None),
        P(None, expert, None, shard),
        P(None, expert, None, shard),
        P(None, expert, None, None),
    )
    return jax.shard_map(
        on_device, mesh=grid, in_specs=in_specs, out_specs=P(None, whole), check_vma=False
    )
```

time: 129 us -> 119 us (0.922)
  Pallas kernels: 18 us -> 34.4 us
  waiting for transfers between devices: 48.3 us -> 34.4 us
  other arithmetic: 8.13 us -> 0.87 us
  local copies, waits for them, and re-layouts: 13.3 us -> 9.38 us
  matrix products: 1.42 us -> 0 us
    pallas_call x4 -> x9, Pallas kernels: 18 us -> 34.4 us  [the longest x2 11.6 us: score(): pl.pallas_call(functools.partial(score_kernel, choice), out_shape=[HALF,...]
    all_to_all x1, waiting for transfers between devices: 11.2 us -> 0.01 us  [on_device(): lax.all_to_all(rows, AXES, 0, 0, axis_index_groups=groups, tiled=True)]
    unnamed x20 -> x22, local copies, waits for them, and re-layouts: 1.29 us -> 7.92 us
    reshape x4 -> x0, local copies, waits for them, and re-layouts: 6.07 us -> none  [the longest x1 2.61 us: on_device(): mine = mine.reshape(256, HIDDEN_SIZE + INNER)]
    ppermute x5, waiting for transfers between devices: 22.9 us -> 17.4 us  [send(): return lax.ppermute(x, ('core', 'xl', 'y'), moves(home_step, guest_step))]
    squeeze x6 -> x0, local copies, waits for them, and re-layouts: 5.17 us -> none  [pick(): return lax.dynamic_index_in_dim(array, which, 0, keepdims=False)[0]]
    concatenate x3 -> x0, other arithmetic: 4.42 us -> none  [the longest x1 3.13 us: on_device(): jnp.concatenate([train_acts.reshape(64, SLOTS, HIDDEN_SIZE), train_grads....]
    select_n x2 -> x0, other arithmetic: 2.83 us -> none  [from_home(): return jnp.where(is_home, x, other_core(x))]
  transfers between devices with their start and end apart: 13 -> 13, of which waited for: 7 -> 7; matrix products, arithmetic and copies ran while one was open for 14% -> 1% of each run, Pallas kernels for 11% -> 22%
where the time goes in v1:
time: 119 us
  starting transfers between devices  39.5 us (33%)
  Pallas kernels  34.4 us (29%)
  waiting for transfers between devices  34.4 us (29%)
  local copies, waits for them, and re-layouts  9.38 us (8%)
    ppermute x5, waiting for transfers between devices, send(): return lax.ppermute(x, ('core', 'xl', 'y'), moves(home_step, guest_step))  17.4 us
    ppermute x5, starting transfers between devices, send(): return lax.ppermute(x, ('core', 'xl', 'y'), moves(home_step, guest_step))  12.2 us
    all_to_all x1, starting transfers between devices, on_device(): lax.all_to_all(rows, AXES, 0, 0, axis_index_groups=groups, tiled=True)  11.9 us
    all_to_all x1, starting transfers between devices, on_device(): lax.all_to_all(mine_sum.reshape(64, SLOTS, QUERIES), AXES, 0, 0, axis_ind...  11.8 us
    pallas_call x2, Pallas kernels, score(): pl.pallas_call(functools.partial(score_kernel, choice), out_shape=[HALF,...  11.6 us
    all_to_all x1, waiting for transfers between devices, on_device(): lax.all_to_all(mine_sum.reshape(64, SLOTS, QUERIES), AXES, 0, 0, axis_ind...  10.5 us
    unnamed x22, local copies, waits for them, and re-layouts  7.92 us
    pallas_call x1, Pallas kernels, score_early(): pl.pallas_call(functools.partial(early_kernel, choice), out_shape=[HALF,...  6.69 us
  transfers between devices with their start and end apart: 13, of which 7 were waited for; matrix products, arithmetic and copies ran while one was open for 1% of the time, Pallas kernels for 22%

profile of v1, /device:TPU:1, one launch (start us, length us, event | category | flops | bytes accessed | tf_op | source)
XLA Modules:
  0.0 118.8 jit_solution(2571805777045345351)
XLA Ops:
  0.0 2.2 %shard_map.91.after = bf16[2816,256]{1,0:T(8,128)(2,1)} custom-call(s32[1]{0:T(128)S(6)} %sub.8.which_ref, bf16[2,1,2048,256]{3,2,1,0:T(8,128)(2,1)} %basis.3, bf16[2,1,768,256]{3,2,1,0:T(8,128)(2,1)} %eigen.3, s32[1]{0:T(128)} %bitcast.1.after.which_ref.turn_ref), custom_call_target="tpu_custom_call" | custom-call | tf_op jit(solution)/shard_map/pallas_call | solution.py:146
  2.2 2.7 %collective-permute-start.1 = (bf16[2816,256]{1,0:T(8,128)(2,1)}, bf16[2816,256]{1,0:T(8,128)(2,1)S(1)}, u32[]{:S(2)}, u32[]{:S(2)}) collective-permute-start(bf16[2816,256]{1,0:T(8,128)(2,1)} %shard_map.91.after), channel_id=1, source_target_pairs={{0,3},{1,2},{2,1},{3,0},{4,8},{5,9},{6,10},{7,11},{8,4},{9,5},{10,... | collective-permute-start | bytes 4325384 | tf_op jit(solution)/shard_map/ppermute | solution.py:71
  5.6 1.9 %collective-permute-start = (bf16[8,256]{1,0:T(8,128)(2,1)S(1)}, bf16[8,256]{1,0:T(8,128)(2,1)S(1)}, u32[]{:S(2)}, u32[]{:S(2)}) collective-permute-start(bf16[8,256]{1,0:T(8,128)(2,1)S(1)} %slice.4), channel_id=1, source_target_pairs={{0,8},{8,0},{1,9},{9,1},{2,10},{10,2},{3,11},{11,3},{4,12},{12,4},... | collective-permute-start | bytes 12296 | tf_op jit(solution)/shard_map/ppermute | solution.py:75
  7.5 0.8 collective-permute-done.after
  8.9 2.2 %shard_map.93.refs_0_ = bf16[2816,256]{1,0:T(8,128)(2,1)} custom-call(s32[1]{0:T(128)} %bitcast.1.after.which_ref.turn_ref, bf16[2,1,2048,256]{3,2,1,0:T(8,128)(2,1)} %basis.3, bf16[2,1,768,256]{3,2,1,0:T(8,128)(2,1)} %eigen.3, bf16[8,256]{1,0:T(8,128)(2,1)} %copy-done.9), custom_call_target="tpu_custom_call" | custom-call | tf_op jit(solution)/shard_map/pallas_call | solution.py:146
  11.1 0.7 collective-permute-start.4
  11.8 2.6 %shard_map.92 = bf16[64,4,2816]{2,1,0:T(4,128)(2,1)} custom-call(bf16[256,2048]{1,0:T(8,128)(2,1)} %acts.1, bf16[256,768]{1,0:T(8,128)(2,1)} %grads.1, bf16[2816,256]{1,0:T(8,128)(2,1)} %shard_map.91.after), custom_call_target="tpu_custom_call" | custom-call | tf_op jit(solution)/shard_map/pallas_call | solution.py:175
  14.4 11.9 %all-to-all-start = ((bf16[64,4,2816]{2,1,0:T(4,128)(2,1)}), bf16[64,4,2816]{2,1,0:T(4,128)(2,1)S(1)}, u32[]{:S(2)}, u32[]{:S(2)}) async-start(bf16[64,4,2816]{2,1,0:T(4,128)(2,1)} %shard_map.92), calls=%async_computation | async-start | bytes 2883584 | tf_op jit(solution)/shard_map/all_to_all | solution.py:431
  26.3 1.1 copy-done
  27.4 3.2 %shard_map.94 = (bf16[64,2048]{1,0:T(8,128)(2,1)}, bf16[848,768]{1,0:T(8,128)(2,1)}) custom-call(s32[1]{0:T(128)} %bitcast.1.after.which_ref.turn_ref, s32[2,1,64]{2,1,0:T(1,128)} %ids.1, bf16[2,1,64,2048]{3,2,1,0:T(8,128)(2,1)} %q_acts.1, bf16[2,1,64,768]{3,2,1,0:T(8,128)(2,1)} %q_grads.1, bf16[2,1,768,768]{3,2,1,0:T(8,128)(2,1)} %b_out.1, ...), custom_call_target="tpu_custom_call" | custom-call | tf_op jit(solution)/shard_map/pallas_call | solution.py:157
  30.6 1.0 collective-permute-start.3
  31.6 2.6 %collective-permute-start.5 = (bf16[2816,256]{1,0:T(8,128)(2,1)}, bf16[2816,256]{1,0:T(8,128)(2,1)S(1)}, u32[]{:S(2)}, u32[]{:S(2)}) collective-permute-start(bf16[2816,256]{1,0:T(8,128)(2,1)} %copy-done), channel_id=1, source_target_pairs={{0,1},{1,0},{2,3},{3,2},{4,7},{5,6},{6,5},{7,4},{8,11},{9,10},{10,... | collective-permute-start | bytes 4325384 | tf_op jit(solution)/shard_map/ppermute | solution.py:71
  34.2 1.7 %collective-permute-done.2.q_other = bf16[64,2048]{1,0:T(8,128)(2,1)S(1)} collective-permute-done((bf16[64,2048]{1,0:T(8,128)(2,1)}, bf16[64,2048]{1,0:T(8,128)(2,1)S(1)}, u32[]{:S(2)}, u32[]{:S(2)}) %collective-permute-start.2) | collective-permute-done | bytes 262176 | tf_op jit(solution)/shard_map/ppermute | solution.py:75
  36.0 0.7 copy-done.7
  36.7 1.3 %copy-done.3 = bf16[848,768]{1,0:T(8,128)(2,1)S(1)} copy-done((bf16[848,768]{1,0:T(8,128)(2,1)S(1)}, bf16[848,768]{1,0:T(8,128)(2,1)}, u32[]{:S(2)}) %copy-start.3) | copy-done | bytes 1302552
  38.0 0.9 copy-done.6
  39.0 0.9 copy-done.8
  39.9 1.8 %shard_map.95 = (bf16[64,2048]{1,0:T(8,128)(2,1)S(1)}, bf16[768,768]{1,0:T(8,128)(2,1)S(1)}, bf16[768,64]{1,0:T(8,128)(2,1)S(1)}, f32[64,128]{1,0:T(8,128)S(1)}) custom-call(s32[1]{0:T(128)} %bitcast.home_ref, bf16[64,2048]{1,0:T(8,128)(2,1)S(1)} %copy-done.6, bf16[64,2048]{1,0:T(8,128)(2,1)S(1)} %copy-done.8, bf16[848,768]{1,0:T(8,128)(2,1)S(1)} %copy-done.3, ...), custom_call_target="tpu_custom_call" | custom-call | flops 75497472 | bytes 5242880 | tf_op jit(solution)/shard_map/pallas_call | solution.py:202
  41.7 1.0 copy-done.4
  42.7 1.5 %collective-permute-done.4.refs_0_ = bf16[2816,256]{1,0:T(8,128)(2,1)} collective-permute-done((bf16[2816,256]{1,0:T(8,128)(2,1)}, bf16[2816,256]{1,0:T(8,128)(2,1)}, u32[]{:S(2)}, u32[]{:S(2)}) %collective-permute-start.4) | collective-permute-done | bytes 1441824 | tf_op jit(solution)/shard_map/ppermute | solution.py:71
  44.3 4.3 %collective-permute-start.6 = (bf16[2816,256]{1,0:T(8,128)(2,1)}, bf16[2816,256]{1,0:T(8,128)(2,1)}, u32[]{:S(2)}, u32[]{:S(2)}) collective-permute-start(bf16[2816,256]{1,0:T(8,128)(2,1)} %collective-permute-done.4.refs_0_), channel_id=1, source_target_pairs={{4,5},{5,4},{6,7},{7,6},{8,9},{9,8},{10,11},{11,10},{20,21},{21,20... | collective-permute-start | bytes 4325384 | tf_op jit(solution)/shard_map/ppermute | solution.py:71
  48.5 15.8 %collective-permute-done.5.refs_1_ = bf16[2816,256]{1,0:T(8,128)(2,1)S(1)} collective-permute-done((bf16[2816,256]{1,0:T(8,128)(2,1)}, bf16[2816,256]{1,0:T(8,128)(2,1)S(1)}, u32[]{:S(2)}, u32[]{:S(2)}) %collective-permute-start.5) | collective-permute-done | bytes 1441824 | tf_op jit(solution)/shard_map/ppermute | solution.py:71
  64.4 1.9 %collective-permute-start.9 = (bf16[2816,256]{1,0:T(8,128)(2,1)S(1)}, bf16[2816,256]{1,0:T(8,128)(2,1)}, u32[]{:S(2)}, u32[]{:S(2)}) collective-permute-start(bf16[2816,256]{1,0:T(8,128)(2,1)S(1)} %collective-permute-done.5.refs_1_), channel_id=1, source_target_pairs={{4,5},{5,4},{6,7},{7,6},{8,9},{9,8},{10,11},{11,10},{20,21},{21,20... | collective-permute-start | bytes 4325384 | tf_op jit(solution)/shard_map/ppermute | solution.py:71
  66.3 1.3 %copy-done.5 = bf16[768,768]{1,0:T(8,128)(2,1)S(1)} copy-done((bf16[768,768]{1,0:T(8,128)(2,1)S(1)}, bf16[768,768]{1,0:T(8,128)(2,1)}, u32[]{:S(2)}) %copy-start.5) | copy-done | bytes 1179672
  67.6 6.7 %shard_map.96 = (f32[256,8]{1,0:T(8,128)S(1)}, bf16[256,2048]{1,0:T(8,128)(2,1)S(1)}, bf16[256,768]{1,0:T(8,128)(2,1)S(1)}, bf16[2,6144,256]{2,1,0:T(8,128)(2,1)S(1)}) custom-call(s32[1]{0:T(128)} %bitcast.home_ref, bf16[64,4,2816]{2,1,0:T(4,128)(2,1)S(1)} %all-to-all-done.rows, bf16[768,768]{1,0:T(8,128)(2,1)S(1)} %copy-done.5, ...), custom_call_target="tpu_custom_call" | custom-call | flops 2 | bytes 2 | tf_op jit(solution)/shard_map/pallas_call | solution.py:351
  74.9 2.7 %collective-permute-done.8.u_ref.u_b = bf16[256,768]{1,0:T(8,128)(2,1)S(1)} collective-permute-done((bf16[256,768]{1,0:T(8,128)(2,1)S(1)}, bf16[256,768]{1,0:T(8,128)(2,1)S(1)}, u32[]{:S(2)}, u32[]{:S(2)}) %collective-permute-start.8) | collective-permute-done | bytes 393248 | tf_op jit(solution)/shard_map/ppermute | solution.py:75
  77.6 4.2 %shard_map.97.sent_in = f32[256,8]{1,0:T(8,128)S(1)} custom-call(bf16[256,2048]{1,0:T(8,128)(2,1)S(1)} %collective-permute-done.7.acts.acts_b, bf16[256,768]{1,0:T(8,128)(2,1)S(1)} %collective-permute-done.8.u_ref.u_b, bf16[2,6144,256]{2,1,0:T(8,128)(2,1)S(1)} %get-tuple-element.40.kept, bf16[2816,256]{1,0:T(8,128)(2,1)} %collective-permute-done.4.refs_0_, ...), custom_call_target="tpu_custom_call" | custom-call | flops 2 | bytes 2 | tf_op jit(solution)/shard_map/pallas_call | solution.py:372
  81.8 5.8 %shard_map.98 = (f32[256,8]{1,0:T(8,128)S(1)}, f32[256,8]{1,0:T(8,128)S(1)}) custom-call(s32[1]{0:T(128)} %bitcast.home_ref, bf16[256,2048]{1,0:T(8,128)(2,1)S(1)} %get-tuple-element.37.acts_a, bf16[256,768]{1,0:T(8,128)(2,1)S(1)} %get-tuple-element.38.u_a, bf16[256,2048]{1,0:T(8,128)(2,1)S(1)} %collective-permute-done.7.acts.acts_b, ...), custom_call_target="tpu_custom_call" | custom-call | flops 1 | bytes 1 | tf_op jit(solution)/shard_map/pallas_call | solution.py:390
  87.7 5.7 %shard_map.99 = (f32[256,8]{1,0:T(8,128)S(1)}, f32[256,8]{1,0:T(8,128)S(1)}) custom-call(s32[1]{0:T(128)} %bitcast.home_ref, bf16[256,2048]{1,0:T(8,128)(2,1)S(1)} %get-tuple-element.37.acts_a, bf16[256,768]{1,0:T(8,128)(2,1)S(1)} %get-tuple-element.38.u_a, bf16[256,2048]{1,0:T(8,128)(2,1)S(1)} %collective-permute-done.7.acts.acts_b, ...), custom_call_target="tpu_custom_call" | custom-call | flops 1 | bytes 1 | tf_op jit(solution)/shard_map/pallas_call | solution.py:390
  93.6 1.2 %collective-permute-done.10 = f32[256,8]{1,0:T(8,128)S(1)} collective-permute-done((f32[256,8]{1,0:T(8,128)S(1)}, f32[256,8]{1,0:T(8,128)S(1)}, u32[]{:S(2)}, u32[]{:S(2)}) %collective-permute-start.10) | collective-permute-done | bytes 8224 | tf_op jit(solution)/shard_map/ppermute | solution.py:75
  95.5 11.8 %all-to-all-start.1 = ((f32[64,4,8]{2,1,0:T(4,128)}), f32[64,4,8]{2,1,0:T(4,128)S(1)}, u32[]{:S(2)}, u32[]{:S(2)}) async-start(f32[64,4,8]{2,1,0:T(4,128)} %bitcast.2), calls=%async_computation.1 | async-start | bytes 262144 | tf_op jit(solution)/shard_map/all_to_all | solution.py:449
  107.5 10.5 %all-to-all-done.1 = f32[64,4,8]{2,1,0:T(4,128)S(1)} async-done(((f32[64,4,8]{2,1,0:T(4,128)}), f32[64,4,8]{2,1,0:T(4,128)S(1)}, u32[]{:S(2)}, u32[]{:S(2)}) %all-to-all-start.1) | async-done | bytes 8224 | tf_op jit(solution)/shard_map/all_to_all | solution.py:449
  (31 shorter events, 3.7 us)
Async XLA Ops:
  2.2 24.1 %collective-permute-start.1 = (bf16[2816,256]{1,0:T(8,128)(2,1)}, bf16[2816,256]{1,0:T(8,128)(2,1)S(1)}, u32[]{:S(2)}, u32[]{:S(2)}) collective-permute-start(bf16[2816,256]{1,0:T(8,128)(2,1)} %shard_map.91.after), channel_id=1, source_target_pairs={{0,3},{1,2},{2,1},{3,0},{4,8},{5,9},{6,10},{7,11},{8,4},{9,5},{10,... | collective-permute-start | bytes 4325384 | tf_op jit(solution)/shard_map/ppermute | solution.py:71
  5.6 2.7 %collective-permute-start = (bf16[8,256]{1,0:T(8,128)(2,1)S(1)}, bf16[8,256]{1,0:T(8,128)(2,1)S(1)}, u32[]{:S(2)}, u32[]{:S(2)}) collective-permute-start(bf16[8,256]{1,0:T(8,128)(2,1)S(1)} %slice.4), channel_id=1, source_target_pairs={{0,8},{8,0},{1,9},{9,1},{2,10},{10,2},{3,11},{11,3},{4,12},{12,4},... | collective-permute-start | bytes 12296 | tf_op jit(solution)/shard_map/ppermute | solution.py:75
  8.3 0.6 copy-start.9
  11.1 33.2 %collective-permute-start.4 = (bf16[2816,256]{1,0:T(8,128)(2,1)}, bf16[2816,256]{1,0:T(8,128)(2,1)}, u32[]{:S(2)}, u32[]{:S(2)}) collective-permute-start(bf16[2816,256]{1,0:T(8,128)(2,1)} %shard_map.93.refs_0_), channel_id=1, source_target_pairs={{0,1},{1,0},{2,3},{3,2},{4,8},{5,9},{6,10},{7,11},{8,4},{9,5},{10,... | collective-permute-start | bytes 4325384 | tf_op jit(solution)/shard_map/ppermute | solution.py:71
  14.4 51.9 %all-to-all-start = ((bf16[64,4,2816]{2,1,0:T(4,128)(2,1)}), bf16[64,4,2816]{2,1,0:T(4,128)(2,1)S(1)}, u32[]{:S(2)}, u32[]{:S(2)}) async-start(bf16[64,4,2816]{2,1,0:T(4,128)(2,1)} %shard_map.92), calls=%async_computation | async-start | bytes 2883584 | tf_op jit(solution)/shard_map/all_to_all | solution.py:431
  26.3 1.1 copy-start
  30.6 6.1 %collective-permute-start.3 = (bf16[848,768]{1,0:T(8,128)(2,1)}, bf16[848,768]{1,0:T(8,128)(2,1)}, u32[]{:S(2)}, u32[]{:S(2)}) collective-permute-start(bf16[848,768]{1,0:T(8,128)(2,1)} %get-tuple-element.28.b_own), channel_id=1, source_target_pairs={{0,8},{8,0},{1,9},{9,1},{2,10},{10,2},{3,11},{11,3},{4,12},{12,4},... | collective-permute-start | bytes 3907592 | tf_op jit(solution)/shard_map/ppermute | solution.py:75
  31.6 32.8 %collective-permute-start.5 = (bf16[2816,256]{1,0:T(8,128)(2,1)}, bf16[2816,256]{1,0:T(8,128)(2,1)S(1)}, u32[]{:S(2)}, u32[]{:S(2)}) collective-permute-start(bf16[2816,256]{1,0:T(8,128)(2,1)} %copy-done), channel_id=1, source_target_pairs={{0,1},{1,0},{2,3},{3,2},{4,7},{5,6},{6,5},{7,4},{8,11},{9,10},{10,... | collective-permute-start | bytes 4325384 | tf_op jit(solution)/shard_map/ppermute | solution.py:71
  34.2 1.7 %collective-permute-start.2 = (bf16[64,2048]{1,0:T(8,128)(2,1)}, bf16[64,2048]{1,0:T(8,128)(2,1)S(1)}, u32[]{:S(2)}, u32[]{:S(2)}) collective-permute-start(bf16[64,2048]{1,0:T(8,128)(2,1)} %get-tuple-element.27.q_own), channel_id=1, source_target_pairs={{0,8},{8,0},{1,9},{9,1},{2,10},{10,2},{3,11},{11,3},{4,12},{12,4},... | collective-permute-start | bytes 786440 | tf_op jit(solution)/shard_map/ppermute | solution.py:75
  36.0 0.7 copy-start.7
  36.7 1.3 %copy-start.3 = (bf16[848,768]{1,0:T(8,128)(2,1)S(1)}, bf16[848,768]{1,0:T(8,128)(2,1)}, u32[]{:S(2)}) copy-start(bf16[848,768]{1,0:T(8,128)(2,1)} %get-tuple-element.28.b_own) | copy-start | bytes 3907588
  38.0 0.9 copy-start.6
  39.0 0.9 copy-start.8
  41.7 1.0 copy-start.4
  44.3 30.0 %collective-permute-start.6 = (bf16[2816,256]{1,0:T(8,128)(2,1)}, bf16[2816,256]{1,0:T(8,128)(2,1)}, u32[]{:S(2)}, u32[]{:S(2)}) collective-permute-start(bf16[2816,256]{1,0:T(8,128)(2,1)} %collective-permute-done.4.refs_0_), channel_id=1, source_target_pairs={{4,5},{5,4},{6,7},{7,6},{8,9},{9,8},{10,11},{11,10},{20,21},{21,20... | collective-permute-start | bytes 4325384 | tf_op jit(solution)/shard_map/ppermute | solution.py:71
  64.4 23.3 %collective-permute-start.9 = (bf16[2816,256]{1,0:T(8,128)(2,1)S(1)}, bf16[2816,256]{1,0:T(8,128)(2,1)}, u32[]{:S(2)}, u32[]{:S(2)}) collective-permute-start(bf16[2816,256]{1,0:T(8,128)(2,1)S(1)} %collective-permute-done.5.refs_1_), channel_id=1, source_target_pairs={{4,5},{5,4},{6,7},{7,6},{8,9},{9,8},{10,11},{11,10},{20,21},{21,20... | collective-permute-start | bytes 4325384 | tf_op jit(solution)/shard_map/ppermute | solution.py:71
  66.3 1.3 %copy-start.5 = (bf16[768,768]{1,0:T(8,128)(2,1)S(1)}, bf16[768,768]{1,0:T(8,128)(2,1)}, u32[]{:S(2)}) copy-start(bf16[768,768]{1,0:T(8,128)(2,1)} %copy-done.4) | copy-start | bytes 3538948
  74.3 3.3 %collective-permute-start.7 = (bf16[256,2048]{1,0:T(8,128)(2,1)S(1)}, bf16[256,2048]{1,0:T(8,128)(2,1)S(1)}, u32[]{:S(2)}, u32[]{:S(2)}) collective-permute-start(bf16[256,2048]{1,0:T(8,128)(2,1)S(1)} %get-tuple-element.37.acts_a), channel_id=1, source_target_pairs={{0,8},{8,0},{1,9},{9,1},{2,10},{10,2},{3,11},{11,3},{4,12},{12,4},... | collective-permute-start | bytes 3145736 | tf_op jit(solution)/shard_map/ppermute | solution.py:75
  74.4 3.2 %collective-permute-start.8 = (bf16[256,768]{1,0:T(8,128)(2,1)S(1)}, bf16[256,768]{1,0:T(8,128)(2,1)S(1)}, u32[]{:S(2)}, u32[]{:S(2)}) collective-permute-start(bf16[256,768]{1,0:T(8,128)(2,1)S(1)} %get-tuple-element.38.u_a), channel_id=1, source_target_pairs={{0,8},{8,0},{1,9},{9,1},{2,10},{10,2},{3,11},{11,3},{4,12},{12,4},... | collective-permute-start | bytes 1179656 | tf_op jit(solution)/shard_map/ppermute | solution.py:75
  77.6 4.2 %copy-start.2 = (bf16[2816,256]{1,0:T(8,128)(2,1)S(1)}, bf16[2816,256]{1,0:T(8,128)(2,1)}, u32[]{:S(2)}) copy-start(bf16[2816,256]{1,0:T(8,128)(2,1)} %shard_map.93.refs_0_) | copy-start | bytes 4325380
  81.8 5.9 %copy-start.1 = (bf16[2816,256]{1,0:T(8,128)(2,1)S(1)}, bf16[2816,256]{1,0:T(8,128)(2,1)}, u32[]{:S(2)}) copy-start(bf16[2816,256]{1,0:T(8,128)(2,1)} %copy-done) | copy-start | bytes 4325380
  87.7 5.9 %copy-start.10 = (s32[1,2,32]{2,1,0:T(2,128)S(1)}, s32[1,2,32]{2,1,0:T(2,128)}, u32[]{:S(2)}) copy-start(s32[1,2,32]{2,1,0:T(2,128)} %param.11) | copy-start | bytes 772
  93.4 1.4 %collective-permute-start.10 = (f32[256,8]{1,0:T(8,128)S(1)}, f32[256,8]{1,0:T(8,128)S(1)}, u32[]{:S(2)}, u32[]{:S(2)}) collective-permute-start(f32[256,8]{1,0:T(8,128)S(1)} %get-tuple-element.46), channel_id=1, source_target_pairs={{0,8},{8,0},{1,9},{9,1},{2,10},{10,2},{3,11},{11,3},{4,12},{12,4},... | collective-permute-start | bytes 24584 | tf_op jit(solution)/shard_map/ppermute | solution.py:75
  95.5 22.4 %all-to-all-start.1 = ((f32[64,4,8]{2,1,0:T(4,128)}), f32[64,4,8]{2,1,0:T(4,128)S(1)}, u32[]{:S(2)}, u32[]{:S(2)}) async-start(f32[64,4,8]{2,1,0:T(4,128)} %bitcast.2), calls=%async_computation.1 | async-start | bytes 262144 | tf_op jit(solution)/shard_map/all_to_all | solution.py:449

commit v2 on v1

--- a/solution.py
+++ b/solution.py
@@ -228,13 +228,29 @@
         pl.when(jnp.logical_not(home))(lambda: act(options[1]))
 
 
+PARTS = [(HIDDEN_SIZE, INNER)] + [(start, 512) for start in range(0, HIDDEN_SIZE, 512)]
+
+
+def start_all(copies):
+    for each in copies:
+        each.start()
+
+
 def fetch_blocks(home, choice, refs, held, sems):
     plan, at = [], 0
     for n, count in enumerate(choice):
         plan.append(
-            [pltpu.make_async_copy(ref, held.at[n], sems.at[n]) for ref in refs[at : at + count]]
+            [
+                [
+                    pltpu.make_async_copy(
+                        ref.at[pl.ds(*part)], held.at[n, pl.ds(*part)], sems.at[n, m]
+                    )
+                    for m, part in enumerate(PARTS)
+                ]
+                for ref in refs[at : at + count]
+            ]
         )
-        each_option(home, plan[n], lambda copy: copy.start())
+        each_option(home, plan[n], start_all)
         at += count
     return plan
 
@@ -244,9 +260,12 @@
     return norm_scale / (held[n, HIDDEN_SIZE:, :].astype(jnp.float32) + DAMPING)
 
 
+def rounded(x):
+    return x.astype(jnp.bfloat16).astype(jnp.float32)
+
+
 def rotate_acts(acts, basis):
-    train_v = jnp.dot(acts, basis, preferred_element_type=jnp.float32)
-    return train_v.astype(jnp.bfloat16).astype(jnp.float32)
+    return rounded(jnp.dot(acts, basis, preferred_element_type=jnp.float32))
 
 
 def precondition(qu_ref, ids_ref, query_v, weight, q):
@@ -264,11 +283,17 @@
 
 def add_blocks(home, plan, held, acts, u_ref, qu_ref, ids_ref, q_acts, total, kept=None):
     for n, options in enumerate(plan):
-        each_option(home, options, lambda copy: copy.wait())
-        basis = held[n, :HIDDEN_SIZE, :]
+        each_option(home, options, lambda copies: copies[0].wait())
         weight = block_weight(held, n)
-        query_v = jnp.dot(q_acts[...], basis, preferred_element_type=jnp.float32)
-        train_v = rotate_acts(acts[...], basis)
+        query_v, train_v = 0.0, 0.0
+        for m, part in enumerate(PARTS[1:]):
+            each_option(home, options, lambda copies: copies[m + 1].wait())
+            basis = held[n, pl.ds(*part), :]
+            query_v += jnp.dot(
+                q_acts[:, pl.ds(*part)], basis, preferred_element_type=jnp.float32
+            )
+            train_v += jnp.dot(acts[:, pl.ds(*part)], basis, preferred_element_type=jnp.float32)
+        train_v = rounded(train_v)
         for q in range(QUERIES):
             precond = precondition(qu_ref, ids_ref, query_v, weight, q)
             if kept is not None:
@@ -298,15 +323,17 @@
     )
 
 
-def late_kernel(acts, u_ref, kept, *refs):
+def late_kernel(acts_a, u_a, acts, u_ref, kept, *refs):
     n_blocks = kept.shape[0]
-    sent_ref, held, sems = refs[n_blocks:]
+    sent_ref, acts_all, u_all, held, sems = refs[n_blocks:]
     copies = [
         pltpu.make_async_copy(ref.at[pl.ds(0, HIDDEN_SIZE)], held.at[n], sems.at[n])
         for n, ref in enumerate(refs[:n_blocks])
     ]
     for each in copies:
         each.start()
+    acts_all[:256], acts_all[256:] = acts_a[...], acts[...]
+    u_all[:256], u_all[256:] = u_a[...], u_ref[...]
     total = jnp.zeros((256, QUERIES), jnp.float32)
     for n, each in enumerate(copies):
         each.wait()
@@ -319,14 +346,12 @@
 
 
 def score_kernel(
-    choice, home_ref, acts_a, u_a, acts_b, u_b, qu_ref, ids_ref, q_acts, mine_in, sent_in, *refs
+    choice, home_ref, acts, u_ref, qu_ref, ids_ref, q_acts, mine_in, sent_in, *refs
 ):
     count = sum(choice)
-    mine_ref, sent_ref, held, acts, u_ref, sems = refs[count:]
+    mine_ref, sent_ref, held, sems = refs[count:]
     home = home_ref[0] == 1
     plan = fetch_blocks(home, choice, refs[:count], held, sems)
-    acts[:256], acts[256:] = acts_a[...], acts_b[...]
-    u_ref[:256], u_ref[256:] = u_a[...], u_b[...]
     total = jnp.concatenate([mine_in[...], sent_in[...]], axis=0)
     total = add_blocks(home, plan, held, acts, u_ref, qu_ref, ids_ref, q_acts, total)
     mine_ref[...] = total[:256]
@@ -360,27 +385,31 @@
         out_specs=[VMEM] * 4,
         scratch_shapes=[
             pltpu.VMEM((n, HIDDEN_SIZE + INNER, 256), jnp.bfloat16),
-            pltpu.SemaphoreType.DMA((n,)),
+            pltpu.SemaphoreType.DMA((n, len(PARTS))),
         ],
         compiler_params=pltpu.CompilerParams(vmem_limit_bytes=28 << 20),
         cost_estimate=score_cost(n),
     )(home, rows, b_out, *queries, *flat)
 
 
-def score_late(acts, u, kept, blocks):
+def score_late(acts_a, u_a, acts_b, u_b, kept, blocks):
     n = len(blocks)
     return pl.pallas_call(
         late_kernel,
-        out_shape=HALF,
-        in_specs=[VMEM] * 3 + [ANY] * n,
-        out_specs=VMEM,
+        out_shape=[
+            HALF,
+            jax.ShapeDtypeStruct((512, HIDDEN_SIZE), jnp.bfloat16),
+            jax.ShapeDtypeStruct((512, INNER), jnp.bfloat16),
+        ],
+        in_specs=[VMEM] * 5 + [ANY] * n,
+        out_specs=[VMEM] * 3,
         scratch_shapes=[
             pltpu.VMEM((n, HIDDEN_SIZE, 256), jnp.bfloat16),
             pltpu.SemaphoreType.DMA((n,)),
         ],
         compiler_params=pltpu.CompilerParams(vmem_limit_bytes=24 << 20),
         cost_estimate=score_cost(n),
-    )(acts, u, kept, *blocks)
+    )(acts_a, u_a, acts_b, u_b, kept, *blocks)
 
 
 def score(home, rows, queries, mine_sum, sent, blocks):
@@ -390,13 +419,11 @@
     return pl.pallas_call(
         functools.partial(score_kernel, choice),
         out_shape=[HALF, HALF],
-        in_specs=[SMEM] + [VMEM] * 9 + [ANY] * len(flat),
+        in_specs=[SMEM] + [VMEM] * 7 + [ANY] * len(flat),
         out_specs=[VMEM] * 2,
         scratch_shapes=[
             pltpu.VMEM((n, HIDDEN_SIZE + INNER, 256), jnp.bfloat16),
-            pltpu.VMEM((512, HIDDEN_SIZE), jnp.bfloat16),
-            pltpu.VMEM((512, INNER), jnp.bfloat16),
-            pltpu.SemaphoreType.DMA((n,)),
+            pltpu.SemaphoreType.DMA((n, len(PARTS))),
         ],
         compiler_params=pltpu.CompilerParams(vmem_limit_bytes=24 << 20),
         cost_estimate=score_cost(n),
@@ -441,8 +468,8 @@
     )
     acts_a, u_a, fourth = lax.optimization_barrier((acts_a, u_a, fourth))
     acts_b, u_b = other_core(acts_a), other_core(u_a)
-    sent = score_late(acts_b, u_b, kept, [second, third])
-    rows = (acts_a, u_a, acts_b, u_b)
+    sent, acts, u = score_late(acts_a, u_a, acts_b, u_b, kept, [second, third])
+    rows = (acts, u)
     for blocks in ([[(own,), (fourth,)]], [[(first,), (fifth,)]]):
         mine_sum, sent = score(home, rows, queries, mine_sum, sent, blocks)
     mine_sum = mine_sum + other_core(sent)

time: 119 us -> 120 us (level)
  Pallas kernels: 34.4 us -> 35.8 us
    pallas_call x1, Pallas kernels: 6.69 us -> 9.28 us  [score_early(): pl.pallas_call(functools.partial(early_kernel, choice), out_shape=[HALF,...]
  transfers between devices with their start and end apart: 13 -> 13, of which waited for: 7 -> 7; matrix products, arithmetic and copies ran while one was open for 1% -> 1% of each run, Pallas kernels for 22% -> 23%
where the time goes in v2:
time: 120 us; the launch traced here: 119 us
  starting transfers between devices  38.9 us (32%)
  Pallas kernels  35.8 us (30%)
  waiting for transfers between devices  34.3 us (29%)
  local copies, waits for them, and re-layouts  9.36 us (8%)
    ppermute x5, waiting for transfers between devices, send(): return lax.ppermute(x, ('core', 'xl', 'y'), moves(home_step, guest_step))  17.3 us
    ppermute x5, starting transfers between devices, send(): return lax.ppermute(x, ('core', 'xl', 'y'), moves(home_step, guest_step))  12.1 us
    all_to_all x1, starting transfers between devices, on_device(): lax.all_to_all(rows, AXES, 0, 0, axis_index_groups=groups, tiled=True)  12.1 us
    pallas_call x2, Pallas kernels, score(): pl.pallas_call(functools.partial(score_kernel, choice), out_shape=[HALF,...  11.4 us
    all_to_all x1, starting transfers between devices, on_device(): lax.all_to_all(mine_sum.reshape(64, SLOTS, QUERIES), AXES, 0, 0, axis_ind...  10.8 us
    all_to_all x1, waiting for transfers between devices, on_device(): lax.all_to_all(mine_sum.reshape(64, SLOTS, QUERIES), AXES, 0, 0, axis_ind...  10.5 us
    pallas_call x1, Pallas kernels, score_early(): pl.pallas_call(functools.partial(early_kernel, choice), out_shape=[HALF,...  9.28 us
    unnamed x22, local copies, waits for them, and re-layouts  7.9 us
  transfers between devices with their start and end apart: 13, of which 7 were waited for; matrix products, arithmetic and copies ran while one was open for 1% of the time, Pallas kernels for 23%

profile of v2, /device:TPU:1, one launch (start us, length us, event | category | flops | bytes accessed | tf_op | source)
XLA Modules:
  0.0 119.5 jit_solution(4121938303392803491)
XLA Ops:
  0.0 2.2 %shard_map.91.after = bf16[2816,256]{1,0:T(8,128)(2,1)} custom-call(s32[1]{0:T(128)S(6)} %sub.8.which_ref, bf16[2,1,2048,256]{3,2,1,0:T(8,128)(2,1)} %basis.3, bf16[2,1,768,256]{3,2,1,0:T(8,128)(2,1)} %eigen.3, s32[1]{0:T(128)} %bitcast.1.after.which_ref.turn_ref), custom_call_target="tpu_custom_call" | custom-call | tf_op jit(solution)/shard_map/pallas_call | solution.py:146
  2.2 2.7 %collective-permute-start.1 = (bf16[2816,256]{1,0:T(8,128)(2,1)}, bf16[2816,256]{1,0:T(8,128)(2,1)S(1)}, u32[]{:S(2)}, u32[]{:S(2)}) collective-permute-start(bf16[2816,256]{1,0:T(8,128)(2,1)} %shard_map.91.after), channel_id=1, source_target_pairs={{0,3},{1,2},{2,1},{3,0},{4,8},{5,9},{6,10},{7,11},{8,4},{9,5},{10,... | collective-permute-start | bytes 4325384 | tf_op jit(solution)/shard_map/ppermute | solution.py:71
  5.6 1.9 %collective-permute-start = (bf16[8,256]{1,0:T(8,128)(2,1)S(1)}, bf16[8,256]{1,0:T(8,128)(2,1)S(1)}, u32[]{:S(2)}, u32[]{:S(2)}) collective-permute-start(bf16[8,256]{1,0:T(8,128)(2,1)S(1)} %slice.4), channel_id=1, source_target_pairs={{0,8},{8,0},{1,9},{9,1},{2,10},{10,2},{3,11},{11,3},{4,12},{12,4},... | collective-permute-start | bytes 12296 | tf_op jit(solution)/shard_map/ppermute | solution.py:75
  7.5 0.8 collective-permute-done.after
  8.9 2.2 %shard_map.93.refs_0_ = bf16[2816,256]{1,0:T(8,128)(2,1)} custom-call(s32[1]{0:T(128)} %bitcast.1.after.which_ref.turn_ref, bf16[2,1,2048,256]{3,2,1,0:T(8,128)(2,1)} %basis.3, bf16[2,1,768,256]{3,2,1,0:T(8,128)(2,1)} %eigen.3, bf16[8,256]{1,0:T(8,128)(2,1)} %copy-done.9), custom_call_target="tpu_custom_call" | custom-call | tf_op jit(solution)/shard_map/pallas_call | solution.py:146
  11.1 0.7 collective-permute-start.4
  11.8 2.6 %shard_map.92 = bf16[64,4,2816]{2,1,0:T(4,128)(2,1)} custom-call(bf16[256,2048]{1,0:T(8,128)(2,1)} %acts.1, bf16[256,768]{1,0:T(8,128)(2,1)} %grads.1, bf16[2816,256]{1,0:T(8,128)(2,1)} %shard_map.91.after), custom_call_target="tpu_custom_call" | custom-call | tf_op jit(solution)/shard_map/pallas_call | solution.py:175
  14.4 12.1 %all-to-all-start = ((bf16[64,4,2816]{2,1,0:T(4,128)(2,1)}), bf16[64,4,2816]{2,1,0:T(4,128)(2,1)}, u32[]{:S(2)}, u32[]{:S(2)}) async-start(bf16[64,4,2816]{2,1,0:T(4,128)(2,1)} %shard_map.92), calls=%async_computation | async-start | bytes 2883584 | tf_op jit(solution)/shard_map/all_to_all | solution.py:458
  26.5 1.1 copy-done
  27.6 3.2 %shard_map.94 = (bf16[64,2048]{1,0:T(8,128)(2,1)}, bf16[848,768]{1,0:T(8,128)(2,1)}) custom-call(s32[1]{0:T(128)} %bitcast.1.after.which_ref.turn_ref, s32[2,1,64]{2,1,0:T(1,128)} %ids.1, bf16[2,1,64,2048]{3,2,1,0:T(8,128)(2,1)} %q_acts.1, bf16[2,1,64,768]{3,2,1,0:T(8,128)(2,1)} %q_grads.1, bf16[2,1,768,768]{3,2,1,0:T(8,128)(2,1)} %b_out.1, ...), custom_call_target="tpu_custom_call" | custom-call | tf_op jit(solution)/shard_map/pallas_call | solution.py:157
  30.9 1.0 collective-permute-start.3
  31.9 2.5 %collective-permute-start.5 = (bf16[2816,256]{1,0:T(8,128)(2,1)}, bf16[2816,256]{1,0:T(8,128)(2,1)S(1)}, u32[]{:S(2)}, u32[]{:S(2)}) collective-permute-start(bf16[2816,256]{1,0:T(8,128)(2,1)} %copy-done), channel_id=1, source_target_pairs={{0,1},{1,0},{2,3},{3,2},{4,7},{5,6},{6,5},{7,4},{8,11},{9,10},{10,... | collective-permute-start | bytes 4325384 | tf_op jit(solution)/shard_map/ppermute | solution.py:71
  34.4 1.7 %collective-permute-done.2.q_other = bf16[64,2048]{1,0:T(8,128)(2,1)S(1)} collective-permute-done((bf16[64,2048]{1,0:T(8,128)(2,1)}, bf16[64,2048]{1,0:T(8,128)(2,1)S(1)}, u32[]{:S(2)}, u32[]{:S(2)}) %collective-permute-start.2) | collective-permute-done | bytes 262176 | tf_op jit(solution)/shard_map/ppermute | solution.py:75
  36.2 0.7 copy-done.7
  36.9 1.3 %copy-done.3 = bf16[848,768]{1,0:T(8,128)(2,1)S(1)} copy-done((bf16[848,768]{1,0:T(8,128)(2,1)S(1)}, bf16[848,768]{1,0:T(8,128)(2,1)}, u32[]{:S(2)}) %copy-start.3) | copy-done | bytes 1302552
  38.2 0.9 copy-done.6
  39.1 0.9 copy-done.8
  40.1 1.8 %shard_map.95 = (bf16[64,2048]{1,0:T(8,128)(2,1)S(1)}, bf16[768,768]{1,0:T(8,128)(2,1)S(1)}, bf16[768,64]{1,0:T(8,128)(2,1)S(1)}, f32[64,128]{1,0:T(8,128)S(1)}) custom-call(s32[1]{0:T(128)} %bitcast.home_ref, bf16[64,2048]{1,0:T(8,128)(2,1)S(1)} %copy-done.6, bf16[64,2048]{1,0:T(8,128)(2,1)S(1)} %copy-done.8, bf16[848,768]{1,0:T(8,128)(2,1)S(1)} %copy-done.3, ...), custom_call_target="tpu_custom_call" | custom-call | flops 75497472 | bytes 5242880 | tf_op jit(solution)/shard_map/pallas_call | solution.py:202
  41.9 1.0 copy-done.4
  42.9 1.5 %collective-permute-done.4.refs_0_ = bf16[2816,256]{1,0:T(8,128)(2,1)S(1)} collective-permute-done((bf16[2816,256]{1,0:T(8,128)(2,1)}, bf16[2816,256]{1,0:T(8,128)(2,1)S(1)}, u32[]{:S(2)}, u32[]{:S(2)}) %collective-permute-start.4) | collective-permute-done | bytes 1441824 | tf_op jit(solution)/shard_map/ppermute | solution.py:71
  44.4 4.3 %collective-permute-start.6 = (bf16[2816,256]{1,0:T(8,128)(2,1)S(1)}, bf16[2816,256]{1,0:T(8,128)(2,1)}, u32[]{:S(2)}, u32[]{:S(2)}) collective-permute-start(bf16[2816,256]{1,0:T(8,128)(2,1)S(1)} %collective-permute-done.4.refs_0_), channel_id=1, source_target_pairs={{4,5},{5,4},{6,7},{7,6},{8,9},{9,8},{10,11},{11,10},{20,21},{21,20... | collective-permute-start | bytes 4325384 | tf_op jit(solution)/shard_map/ppermute | solution.py:71
  48.7 15.8 %collective-permute-done.5.refs_1_ = bf16[2816,256]{1,0:T(8,128)(2,1)S(1)} collective-permute-done((bf16[2816,256]{1,0:T(8,128)(2,1)}, bf16[2816,256]{1,0:T(8,128)(2,1)S(1)}, u32[]{:S(2)}, u32[]{:S(2)}) %collective-permute-start.5) | collective-permute-done | bytes 1441824 | tf_op jit(solution)/shard_map/ppermute | solution.py:71
  64.5 1.9 %collective-permute-start.9 = (bf16[2816,256]{1,0:T(8,128)(2,1)S(1)}, bf16[2816,256]{1,0:T(8,128)(2,1)}, u32[]{:S(2)}, u32[]{:S(2)}) collective-permute-start(bf16[2816,256]{1,0:T(8,128)(2,1)S(1)} %collective-permute-done.5.refs_1_), channel_id=1, source_target_pairs={{4,5},{5,4},{6,7},{7,6},{8,9},{9,8},{10,11},{11,10},{20,21},{21,20... | collective-permute-start | bytes 4325384 | tf_op jit(solution)/shard_map/ppermute | solution.py:71
  66.4 1.3 %copy-done.5 = bf16[768,768]{1,0:T(8,128)(2,1)S(1)} copy-done((bf16[768,768]{1,0:T(8,128)(2,1)S(1)}, bf16[768,768]{1,0:T(8,128)(2,1)}, u32[]{:S(2)}) %copy-start.5) | copy-done | bytes 1179672
  67.7 9.3 %shard_map.96 = (f32[256,8]{1,0:T(8,128)S(1)}, bf16[256,2048]{1,0:T(8,128)(2,1)S(1)}, bf16[256,768]{1,0:T(8,128)(2,1)S(1)}, bf16[2,6144,256]{2,1,0:T(8,128)(2,1)S(1)}) custom-call(s32[1]{0:T(128)} %bitcast.home_ref, bf16[64,4,2816]{2,1,0:T(4,128)(2,1)} %all-to-all-done.rows, bf16[768,768]{1,0:T(8,128)(2,1)S(1)} %copy-done.5, ...), custom_call_target="tpu_custom_call" | custom-call | flops 2 | bytes 2 | tf_op jit(solution)/shard_map/pallas_call | solution.py:376
  77.8 2.7 %collective-permute-done.8.u_ref = bf16[256,768]{1,0:T(8,128)(2,1)S(1)} collective-permute-done((bf16[256,768]{1,0:T(8,128)(2,1)S(1)}, bf16[256,768]{1,0:T(8,128)(2,1)S(1)}, u32[]{:S(2)}, u32[]{:S(2)}) %collective-permute-start.8) | collective-permute-done | bytes 393248 | tf_op jit(solution)/shard_map/ppermute | solution.py:75
  80.5 3.2 %shard_map.97 = (f32[256,8]{1,0:T(8,128)S(1)}, bf16[512,2048]{1,0:T(8,128)(2,1)S(1)}, bf16[512,768]{1,0:T(8,128)(2,1)S(1)}) custom-call(bf16[256,2048]{1,0:T(8,128)(2,1)S(1)} %get-tuple-element.40.acts_a, bf16[256,768]{1,0:T(8,128)(2,1)S(1)} %get-tuple-element.41.u_a, bf16[256,2048]{1,0:T(8,128)(2,1)S(1)} %collective-permute-done.7.acts, ...), custom_call_target="tpu_custom_call" | custom-call | flops 2 | bytes 2 | tf_op jit(solution)/shard_map/pallas_call | solution.py:397
  83.7 5.8 %shard_map.98 = (f32[256,8]{1,0:T(8,128)S(1)}, f32[256,8]{1,0:T(8,128)S(1)}) custom-call(s32[1]{0:T(128)} %bitcast.home_ref, bf16[512,2048]{1,0:T(8,128)(2,1)S(1)} %get-tuple-element.43.acts, bf16[512,768]{1,0:T(8,128)(2,1)S(1)} %get-tuple-element.44.u_ref, bf16[768,64]{1,0:T(8,128)(2,1)S(1)} %get-tuple-element.34.qu_ref, ...), custom_call_target="tpu_custom_call" | custom-call | flops 1 | bytes 1 | tf_op jit(solution)/shard_map/pallas_call | solution.py:419
  89.5 5.7 %shard_map.99 = (f32[256,8]{1,0:T(8,128)S(1)}, f32[256,8]{1,0:T(8,128)S(1)}) custom-call(s32[1]{0:T(128)} %bitcast.home_ref, bf16[512,2048]{1,0:T(8,128)(2,1)S(1)} %get-tuple-element.43.acts, bf16[512,768]{1,0:T(8,128)(2,1)S(1)} %get-tuple-element.44.u_ref, bf16[768,64]{1,0:T(8,128)(2,1)S(1)} %get-tuple-element.34.qu_ref, ...), custom_call_target="tpu_custom_call" | custom-call | flops 1 | bytes 1 | tf_op jit(solution)/shard_map/pallas_call | solution.py:419
  95.4 1.2 %collective-permute-done.10 = f32[256,8]{1,0:T(8,128)S(1)} collective-permute-done((f32[256,8]{1,0:T(8,128)S(1)}, f32[256,8]{1,0:T(8,128)S(1)}, u32[]{:S(2)}, u32[]{:S(2)}) %collective-permute-start.10) | collective-permute-done | bytes 8224 | tf_op jit(solution)/shard_map/ppermute | solution.py:75
  97.3 10.8 %all-to-all-start.1 = ((f32[64,4,8]{2,1,0:T(4,128)}), f32[64,4,8]{2,1,0:T(4,128)S(1)}, u32[]{:S(2)}, u32[]{:S(2)}) async-start(f32[64,4,8]{2,1,0:T(4,128)} %bitcast.2), calls=%async_computation.1 | async-start | bytes 262144 | tf_op jit(solution)/shard_map/all_to_all | solution.py:476
  108.2 10.5 %all-to-all-done.1 = f32[64,4,8]{2,1,0:T(4,128)S(1)} async-done(((f32[64,4,8]{2,1,0:T(4,128)}), f32[64,4,8]{2,1,0:T(4,128)S(1)}, u32[]{:S(2)}, u32[]{:S(2)}) %all-to-all-start.1) | async-done | bytes 8224 | tf_op jit(solution)/shard_map/all_to_all | solution.py:476
  (31 shorter events, 3.8 us)
Async XLA Ops:
  2.2 24.3 %collective-permute-start.1 = (bf16[2816,256]{1,0:T(8,128)(2,1)}, bf16[2816,256]{1,0:T(8,128)(2,1)S(1)}, u32[]{:S(2)}, u32[]{:S(2)}) collective-permute-start(bf16[2816,256]{1,0:T(8,128)(2,1)} %shard_map.91.after), channel_id=1, source_target_pairs={{0,3},{1,2},{2,1},{3,0},{4,8},{5,9},{6,10},{7,11},{8,4},{9,5},{10,... | collective-permute-start | bytes 4325384 | tf_op jit(solution)/shard_map/ppermute | solution.py:71
  5.6 2.7 %collective-permute-start = (bf16[8,256]{1,0:T(8,128)(2,1)S(1)}, bf16[8,256]{1,0:T(8,128)(2,1)S(1)}, u32[]{:S(2)}, u32[]{:S(2)}) collective-permute-start(bf16[8,256]{1,0:T(8,128)(2,1)S(1)} %slice.4), channel_id=1, source_target_pairs={{0,8},{8,0},{1,9},{9,1},{2,10},{10,2},{3,11},{11,3},{4,12},{12,4},... | collective-permute-start | bytes 12296 | tf_op jit(solution)/shard_map/ppermute | solution.py:75
  8.3 0.6 copy-start.9
  11.1 33.3 %collective-permute-start.4 = (bf16[2816,256]{1,0:T(8,128)(2,1)}, bf16[2816,256]{1,0:T(8,128)(2,1)S(1)}, u32[]{:S(2)}, u32[]{:S(2)}) collective-permute-start(bf16[2816,256]{1,0:T(8,128)(2,1)} %shard_map.93.refs_0_), channel_id=1, source_target_pairs={{0,1},{1,0},{2,3},{3,2},{4,8},{5,9},{6,10},{7,11},{8,4},{9,5},{10,... | collective-permute-start | bytes 4325384 | tf_op jit(solution)/shard_map/ppermute | solution.py:71
  14.4 52.0 %all-to-all-start = ((bf16[64,4,2816]{2,1,0:T(4,128)(2,1)}), bf16[64,4,2816]{2,1,0:T(4,128)(2,1)}, u32[]{:S(2)}, u32[]{:S(2)}) async-start(bf16[64,4,2816]{2,1,0:T(4,128)(2,1)} %shard_map.92), calls=%async_computation | async-start | bytes 2883584 | tf_op jit(solution)/shard_map/all_to_all | solution.py:458
  26.5 1.1 copy-start
  30.9 6.0 %collective-permute-start.3 = (bf16[848,768]{1,0:T(8,128)(2,1)}, bf16[848,768]{1,0:T(8,128)(2,1)}, u32[]{:S(2)}, u32[]{:S(2)}) collective-permute-start(bf16[848,768]{1,0:T(8,128)(2,1)} %get-tuple-element.31.b_own), channel_id=1, source_target_pairs={{0,8},{8,0},{1,9},{9,1},{2,10},{10,2},{3,11},{11,3},{4,12},{12,4},... | collective-permute-start | bytes 3907592 | tf_op jit(solution)/shard_map/ppermute | solution.py:75
  31.9 32.6 %collective-permute-start.5 = (bf16[2816,256]{1,0:T(8,128)(2,1)}, bf16[2816,256]{1,0:T(8,128)(2,1)S(1)}, u32[]{:S(2)}, u32[]{:S(2)}) collective-permute-start(bf16[2816,256]{1,0:T(8,128)(2,1)} %copy-done), channel_id=1, source_target_pairs={{0,1},{1,0},{2,3},{3,2},{4,7},{5,6},{6,5},{7,4},{8,11},{9,10},{10,... | collective-permute-start | bytes 4325384 | tf_op jit(solution)/shard_map/ppermute | solution.py:71
  34.4 1.7 %collective-permute-start.2 = (bf16[64,2048]{1,0:T(8,128)(2,1)}, bf16[64,2048]{1,0:T(8,128)(2,1)S(1)}, u32[]{:S(2)}, u32[]{:S(2)}) collective-permute-start(bf16[64,2048]{1,0:T(8,128)(2,1)} %get-tuple-element.30.q_own), channel_id=1, source_target_pairs={{0,8},{8,0},{1,9},{9,1},{2,10},{10,2},{3,11},{11,3},{4,12},{12,4},... | collective-permute-start | bytes 786440 | tf_op jit(solution)/shard_map/ppermute | solution.py:75
  36.1 0.7 copy-start.7
  36.9 1.3 %copy-start.3 = (bf16[848,768]{1,0:T(8,128)(2,1)S(1)}, bf16[848,768]{1,0:T(8,128)(2,1)}, u32[]{:S(2)}) copy-start(bf16[848,768]{1,0:T(8,128)(2,1)} %get-tuple-element.31.b_own) | copy-start | bytes 3907588
  38.2 0.9 copy-start.6
  39.1 0.9 copy-start.8
  41.9 1.0 copy-start.4
  44.4 32.6 %collective-permute-start.6 = (bf16[2816,256]{1,0:T(8,128)(2,1)S(1)}, bf16[2816,256]{1,0:T(8,128)(2,1)}, u32[]{:S(2)}, u32[]{:S(2)}) collective-permute-start(bf16[2816,256]{1,0:T(8,128)(2,1)S(1)} %collective-permute-done.4.refs_0_), channel_id=1, source_target_pairs={{4,5},{5,4},{6,7},{7,6},{8,9},{9,8},{10,11},{11,10},{20,21},{21,20... | collective-permute-start | bytes 4325384 | tf_op jit(solution)/shard_map/ppermute | solution.py:71
  64.5 25.0 %collective-permute-start.9 = (bf16[2816,256]{1,0:T(8,128)(2,1)S(1)}, bf16[2816,256]{1,0:T(8,128)(2,1)}, u32[]{:S(2)}, u32[]{:S(2)}) collective-permute-start(bf16[2816,256]{1,0:T(8,128)(2,1)S(1)} %collective-permute-done.5.refs_1_), channel_id=1, source_target_pairs={{4,5},{5,4},{6,7},{7,6},{8,9},{9,8},{10,11},{11,10},{20,21},{21,20... | collective-permute-start | bytes 4325384 | tf_op jit(solution)/shard_map/ppermute | solution.py:71
  66.4 1.3 %copy-start.5 = (bf16[768,768]{1,0:T(8,128)(2,1)S(1)}, bf16[768,768]{1,0:T(8,128)(2,1)}, u32[]{:S(2)}) copy-start(bf16[768,768]{1,0:T(8,128)(2,1)} %copy-done.4) | copy-start | bytes 3538948
  77.0 3.5 %collective-permute-start.7 = (bf16[256,2048]{1,0:T(8,128)(2,1)S(1)}, bf16[256,2048]{1,0:T(8,128)(2,1)S(1)}, u32[]{:S(2)}, u32[]{:S(2)}) collective-permute-start(bf16[256,2048]{1,0:T(8,128)(2,1)S(1)} %get-tuple-element.40.acts_a), channel_id=1, source_target_pairs={{0,8},{8,0},{1,9},{9,1},{2,10},{10,2},{3,11},{11,3},{4,12},{12,4},... | collective-permute-start | bytes 3145736 | tf_op jit(solution)/shard_map/ppermute | solution.py:75
  77.3 3.2 %collective-permute-start.8 = (bf16[256,768]{1,0:T(8,128)(2,1)S(1)}, bf16[256,768]{1,0:T(8,128)(2,1)S(1)}, u32[]{:S(2)}, u32[]{:S(2)}) collective-permute-start(bf16[256,768]{1,0:T(8,128)(2,1)S(1)} %get-tuple-element.41.u_a), channel_id=1, source_target_pairs={{0,8},{8,0},{1,9},{9,1},{2,10},{10,2},{3,11},{11,3},{4,12},{12,4},... | collective-permute-start | bytes 1179656 | tf_op jit(solution)/shard_map/ppermute | solution.py:75
  80.5 3.2 %copy-start.2 = (bf16[2816,256]{1,0:T(8,128)(2,1)S(1)}, bf16[2816,256]{1,0:T(8,128)(2,1)}, u32[]{:S(2)}) copy-start(bf16[2816,256]{1,0:T(8,128)(2,1)} %shard_map.93.refs_0_) | copy-start | bytes 4325380
  83.7 5.8 %copy-start.1 = (bf16[2816,256]{1,0:T(8,128)(2,1)S(1)}, bf16[2816,256]{1,0:T(8,128)(2,1)}, u32[]{:S(2)}) copy-start(bf16[2816,256]{1,0:T(8,128)(2,1)} %copy-done) | copy-start | bytes 4325380
  89.5 5.8 %copy-start.10 = (s32[1,2,32]{2,1,0:T(2,128)S(1)}, s32[1,2,32]{2,1,0:T(2,128)}, u32[]{:S(2)}) copy-start(s32[1,2,32]{2,1,0:T(2,128)} %param.11) | copy-start | bytes 772
  95.2 1.4 %collective-permute-start.10 = (f32[256,8]{1,0:T(8,128)S(1)}, f32[256,8]{1,0:T(8,128)S(1)}, u32[]{:S(2)}, u32[]{:S(2)}) collective-permute-start(f32[256,8]{1,0:T(8,128)S(1)} %get-tuple-element.52), channel_id=1, source_target_pairs={{0,8},{8,0},{1,9},{9,1},{2,10},{10,2},{3,11},{11,3},{4,12},{12,4},... | collective-permute-start | bytes 24584 | tf_op jit(solution)/shard_map/ppermute | solution.py:75
  97.3 21.4 %all-to-all-start.1 = ((f32[64,4,8]{2,1,0:T(4,128)}), f32[64,4,8]{2,1,0:T(4,128)S(1)}, u32[]{:S(2)}, u32[]{:S(2)}) async-start(f32[64,4,8]{2,1,0:T(4,128)} %bitcast.2), calls=%async_computation.1 | async-start | bytes 262144 | tf_op jit(solution)/shard_map/all_to_all | solution.py:476

commit v3 on v1

--- a/solution.py
+++ b/solution.py
@@ -40,6 +40,20 @@
     return groups
 
 
+def return_groups():
+    return [
+        [
+            flat_index(xh, z, core, xl, (low, 3 - low)[k])
+            for core in range(2)
+            for k in range(2)
+            for xh in range(2)
+            for z in range(8)
+            for xl in range(2)
+        ]
+        for low in range(2)
+    ]
+
+
 def moves(home_step, guest_step):
     pairs = []
     for core in range(2):
@@ -298,15 +312,17 @@
     )
 
 
-def late_kernel(acts, u_ref, kept, *refs):
+def late_kernel(acts_a, u_a, acts, u_ref, kept, *refs):
     n_blocks = kept.shape[0]
-    sent_ref, held, sems = refs[n_blocks:]
+    sent_ref, acts_all, u_all, held, sems = refs[n_blocks:]
     copies = [
         pltpu.make_async_copy(ref.at[pl.ds(0, HIDDEN_SIZE)], held.at[n], sems.at[n])
         for n, ref in enumerate(refs[:n_blocks])
     ]
     for each in copies:
         each.start()
+    acts_all[:256], acts_all[256:] = acts_a[...], acts[...]
+    u_all[:256], u_all[256:] = u_a[...], u_ref[...]
     total = jnp.zeros((256, QUERIES), jnp.float32)
     for n, each in enumerate(copies):
         each.wait()
@@ -319,21 +335,25 @@
 
 
 def score_kernel(
-    choice, home_ref, acts_a, u_a, acts_b, u_b, qu_ref, ids_ref, q_acts, mine_in, sent_in, *refs
+    choice, last, home_ref, acts, u_ref, qu_ref, ids_ref, q_acts, mine_in, sent_in, *refs
 ):
     count = sum(choice)
-    mine_ref, sent_ref, held, acts, u_ref, sems = refs[count:]
+    *out_refs, held, sems = refs[count:]
     home = home_ref[0] == 1
     plan = fetch_blocks(home, choice, refs[:count], held, sems)
-    acts[:256], acts[256:] = acts_a[...], acts_b[...]
-    u_ref[:256], u_ref[256:] = u_a[...], u_b[...]
     total = jnp.concatenate([mine_in[...], sent_in[...]], axis=0)
     total = add_blocks(home, plan, held, acts, u_ref, qu_ref, ids_ref, q_acts, total)
-    mine_ref[...] = total[:256]
-    sent_ref[...] = total[256:]
+    if last:
+        core = home_ref[1]
+        out_refs[0][core] = total[:256]
+        out_refs[0][1 - core] = total[256:]
+    else:
+        out_refs[0][...] = total[:256]
+        out_refs[1][...] = total[256:]
 
 
 HALF = jax.ShapeDtypeStruct((256, QUERIES), jnp.float32)
+BOTH = jax.ShapeDtypeStruct((2, 256, QUERIES), jnp.float32)
 
 
 def score_cost(n):
@@ -367,35 +387,37 @@
     )(home, rows, b_out, *queries, *flat)
 
 
-def score_late(acts, u, kept, blocks):
+def score_late(acts_a, u_a, acts_b, u_b, kept, blocks):
     n = len(blocks)
     return pl.pallas_call(
         late_kernel,
-        out_shape=HALF,
-        in_specs=[VMEM] * 3 + [ANY] * n,
-        out_specs=VMEM,
+        out_shape=[
+            HALF,
+            jax.ShapeDtypeStruct((512, HIDDEN_SIZE), jnp.bfloat16),
+            jax.ShapeDtypeStruct((512, INNER), jnp.bfloat16),
+        ],
+        in_specs=[VMEM] * 5 + [ANY] * n,
+        out_specs=[VMEM] * 3,
         scratch_shapes=[
             pltpu.VMEM((n, HIDDEN_SIZE, 256), jnp.bfloat16),
             pltpu.SemaphoreType.DMA((n,)),
         ],
         compiler_params=pltpu.CompilerParams(vmem_limit_bytes=24 << 20),
         cost_estimate=score_cost(n),
-    )(acts, u, kept, *blocks)
-
-
-def score(home, rows, queries, mine_sum, sent, blocks):
+    )(acts_a, u_a, acts_b, u_b, kept, *blocks)
+
+
+def score(home, rows, queries, mine_sum, sent, blocks, last):
     choice = tuple(len(options) for options in blocks)
     flat = [x for options in blocks for (x,) in options]
     n = len(blocks)
     return pl.pallas_call(
-        functools.partial(score_kernel, choice),
-        out_shape=[HALF, HALF],
-        in_specs=[SMEM] + [VMEM] * 9 + [ANY] * len(flat),
-        out_specs=[VMEM] * 2,
+        functools.partial(score_kernel, choice, last),
+        out_shape=[BOTH] if last else [HALF, HALF],
+        in_specs=[SMEM] + [VMEM] * 7 + [ANY] * len(flat),
+        out_specs=[VMEM] if last else [VMEM] * 2,
         scratch_shapes=[
             pltpu.VMEM((n, HIDDEN_SIZE + INNER, 256), jnp.bfloat16),
-            pltpu.VMEM((512, HIDDEN_SIZE), jnp.bfloat16),
-            pltpu.VMEM((512, INNER), jnp.bfloat16),
             pltpu.SemaphoreType.DMA((n,)),
         ],
         compiler_params=pltpu.CompilerParams(vmem_limit_bytes=24 << 20),
@@ -417,7 +439,7 @@
     core, xl, y = lax.axis_index("core"), lax.axis_index("xl"), lax.axis_index("y")
     turn = y // 2
     is_home = core == xl
-    home = is_home.astype(jnp.int32).reshape(1)
+    home = jnp.stack([is_home.astype(jnp.int32), core.astype(jnp.int32)])
     groups = route_groups()
 
     turn_ref = turn.astype(jnp.int32).reshape(1)
@@ -435,23 +457,31 @@
     q_acts, b_out, qu, ids = query(home, q_own, other_core(q_own), b_own, other_core(b_own))
     held_second, qu = lax.optimization_barrier((second, qu))
     fourth = send(held_second, None, inner_step)
+    counts = slot_counts[0].reshape(64)
+    live = (jnp.arange(SLOTS)[None, :] < counts[:, None]).astype(jnp.float32)
+    live, qu = lax.optimization_barrier((live, qu))
     queries = (qu, ids, q_acts)
     mine_sum, acts_a, u_a, kept = score_early(
         home, mine, b_out, queries, [[(second,)], [(third,)]]
     )
     acts_a, u_a, fourth = lax.optimization_barrier((acts_a, u_a, fourth))
     acts_b, u_b = other_core(acts_a), other_core(u_a)
-    sent = score_late(acts_b, u_b, kept, [second, third])
-    rows = (acts_a, u_a, acts_b, u_b)
-    for blocks in ([[(own,), (fourth,)]], [[(first,), (fifth,)]]):
-        mine_sum, sent = score(home, rows, queries, mine_sum, sent, blocks)
-    mine_sum = mine_sum + other_core(sent)
+    sent, acts, u = score_late(acts_a, u_a, acts_b, u_b, kept, [second, third])
+    rows = (acts, u)
+    mine_sum, sent = score(
+        home, rows, queries, mine_sum, sent, [[(own,), (fourth,)]], False
+    )
+    (both,) = score(home, rows, queries, mine_sum, sent, [[(first,), (fifth,)]], True)
     back = lax.all_to_all(
-        mine_sum.reshape(64, SLOTS, QUERIES), AXES, 0, 0, axis_index_groups=groups, tiled=True
-    )
-    counts = slot_counts[0].reshape(64)
-    live = jnp.arange(SLOTS)[None, :] < counts[:, None]
-    return jnp.where(live[:, :, None], back, 0.0).reshape(256, QUERIES).T
+        both.reshape(128, SLOTS, QUERIES),
+        AXES,
+        0,
+        0,
+        axis_index_groups=return_groups(),
+        tiled=True,
+    )
+    back = back[:64] + back[64:]
+    return jnp.where(live[:, :, None] > 0, back, 0.0).reshape(256, QUERIES).T
 
 
 def solution(mesh):

time: 119 us -> 123 us (1.034)
  Pallas kernels: 34.4 us -> 36.9 us
  waiting for transfers between devices: 34.4 us -> 35.7 us
    all_to_all x1, waiting for transfers between devices: 10.5 us -> 13.8 us  [on_device(): lax.all_to_all(both.reshape(128, SLOTS, QUERIES), AXES, 0, 0, axis_index_...]
    ppermute x6 -> x5, waiting for transfers between devices: 6.53 us -> 5.21 us  [other_core(): return lax.ppermute(x, 'core', [(0, 1), (1, 0)])]
    pallas_call x1, Pallas kernels: 6.69 us -> 7.95 us  [score_early(): pl.pallas_call(functools.partial(early_kernel, choice), out_shape=[HALF,...]
    ppermute x6 -> x5, starting transfers between devices: 3.61 us -> 3.52 us  [other_core(): return lax.ppermute(x, 'core', [(0, 1), (1, 0)])]
  transfers between devices with their start and end apart: 13 -> 12, of which waited for: 7 -> 6; matrix products, arithmetic and copies ran while one was open for 1% -> 1% of each run, Pallas kernels for 22% -> 23%
where the time goes in v3:
time: 123 us; the launch traced here: 122 us
  starting transfers between devices  39.9 us (32%)
  Pallas kernels  36.9 us (30%)
  waiting for transfers between devices  35.7 us (29%)
  local copies, waits for them, and re-layouts  9.36 us (8%)
    ppermute x5, waiting for transfers between devices, send(): return lax.ppermute(x, ('core', 'xl', 'y'), moves(home_step, guest_step))  16.8 us
    all_to_all x1, waiting for transfers between devices, on_device(): lax.all_to_all(both.reshape(128, SLOTS, QUERIES), AXES, 0, 0, axis_index_...  13.8 us
    pallas_call x2, Pallas kernels, score(): pl.pallas_call(functools.partial(score_kernel, choice, last), out_shape=[...  13.3 us
    ppermute x5, starting transfers between devices, send(): return lax.ppermute(x, ('core', 'xl', 'y'), moves(home_step, guest_step))  12.2 us
    all_to_all x1, starting transfers between devices, on_device(): lax.all_to_all(both.reshape(128, SLOTS, QUERIES), AXES, 0, 0, axis_index_...  12.1 us
    all_to_all x1, starting transfers between devices, on_device(): lax.all_to_all(rows, AXES, 0, 0, axis_index_groups=groups, tiled=True)  12.1 us
    pallas_call x1, Pallas kernels, score_early(): pl.pallas_call(functools.partial(early_kernel, choice), out_shape=[HALF,...  7.95 us
    unnamed x22, local copies, waits for them, and re-layouts  7.9 us
  transfers between devices with their start and end apart: 12, of which 6 were waited for; matrix products, arithmetic and copies ran while one was open for 1% of the time, Pallas kernels for 23%

profile of v3, /device:TPU:1, one launch (start us, length us, event | category | flops | bytes accessed | tf_op | source)
XLA Modules:
  0.0 122.4 jit_solution(11775633711315464616)
XLA Ops:
  0.0 2.2 %shard_map.91.after = bf16[2816,256]{1,0:T(8,128)(2,1)} custom-call(s32[1]{0:T(128)S(6)} %sub.8.which_ref, bf16[2,1,2048,256]{3,2,1,0:T(8,128)(2,1)} %basis.3, bf16[2,1,768,256]{3,2,1,0:T(8,128)(2,1)} %eigen.3, s32[1]{0:T(128)} %bitcast.after.which_ref.turn_ref), custom_call_target="tpu_custom_call" | custom-call | tf_op jit(solution)/shard_map/pallas_call | solution.py:160
  2.2 2.7 %collective-permute-start.2 = (bf16[2816,256]{1,0:T(8,128)(2,1)}, bf16[2816,256]{1,0:T(8,128)(2,1)S(1)}, u32[]{:S(2)}, u32[]{:S(2)}) collective-permute-start(bf16[2816,256]{1,0:T(8,128)(2,1)} %shard_map.91.after), channel_id=1, source_target_pairs={{0,3},{1,2},{2,1},{3,0},{4,8},{5,9},{6,10},{7,11},{8,4},{9,5},{10,... | collective-permute-start | bytes 4325384 | tf_op jit(solution)/shard_map/ppermute | solution.py:85
  4.9 0.7 slice.12
  5.6 1.9 %collective-permute-start = (bf16[8,256]{1,0:T(8,128)(2,1)S(1)}, bf16[8,256]{1,0:T(8,128)(2,1)S(1)}, u32[]{:S(2)}, u32[]{:S(2)}) collective-permute-start(bf16[8,256]{1,0:T(8,128)(2,1)S(1)} %slice.12), channel_id=1, source_target_pairs={{0,8},{8,0},{1,9},{9,1},{2,10},{10,2},{3,11},{11,3},{4,12},{12,4},... | collective-permute-start | bytes 12296 | tf_op jit(solution)/shard_map/ppermute | solution.py:89
  7.5 0.8 collective-permute-done.after
  8.9 2.2 %shard_map.92.refs_0_ = bf16[2816,256]{1,0:T(8,128)(2,1)} custom-call(s32[1]{0:T(128)} %bitcast.after.which_ref.turn_ref, bf16[2,1,2048,256]{3,2,1,0:T(8,128)(2,1)} %basis.3, bf16[2,1,768,256]{3,2,1,0:T(8,128)(2,1)} %eigen.3, bf16[8,256]{1,0:T(8,128)(2,1)} %copy-done.9), custom_call_target="tpu_custom_call" | custom-call | tf_op jit(solution)/shard_map/pallas_call | solution.py:160
  11.1 0.7 collective-permute-start.1
  11.8 2.6 %shard_map.95 = bf16[64,4,2816]{2,1,0:T(4,128)(2,1)} custom-call(bf16[256,2048]{1,0:T(8,128)(2,1)} %acts.1, bf16[256,768]{1,0:T(8,128)(2,1)} %grads.1, bf16[2816,256]{1,0:T(8,128)(2,1)} %shard_map.91.after), custom_call_target="tpu_custom_call" | custom-call | tf_op jit(solution)/shard_map/pallas_call | solution.py:189
  14.4 12.1 %all-to-all-start = ((bf16[64,4,2816]{2,1,0:T(4,128)(2,1)}), bf16[64,4,2816]{2,1,0:T(4,128)(2,1)}, u32[]{:S(2)}, u32[]{:S(2)}) async-start(bf16[64,4,2816]{2,1,0:T(4,128)(2,1)} %shard_map.95), calls=%async_computation | async-start | bytes 2883584 | tf_op jit(solution)/shard_map/all_to_all | solution.py:453
  26.5 1.1 copy-done.1
  27.6 3.2 %shard_map.93 = (bf16[64,2048]{1,0:T(8,128)(2,1)}, bf16[848,768]{1,0:T(8,128)(2,1)}) custom-call(s32[1]{0:T(128)} %bitcast.after.which_ref.turn_ref, s32[2,1,64]{2,1,0:T(1,128)} %ids.1, bf16[2,1,64,2048]{3,2,1,0:T(8,128)(2,1)} %q_acts.1, bf16[2,1,64,768]{3,2,1,0:T(8,128)(2,1)} %q_grads.1, bf16[2,1,768,768]{3,2,1,0:T(8,128)(2,1)} %b_out.1, ...), custom_call_target="tpu_custom_call" | custom-call | tf_op jit(solution)/shard_map/pallas_call | solution.py:171
  30.8 1.0 collective-permute-start.4
  31.8 2.5 %collective-permute-start.5 = (bf16[2816,256]{1,0:T(8,128)(2,1)}, bf16[2816,256]{1,0:T(8,128)(2,1)S(1)}, u32[]{:S(2)}, u32[]{:S(2)}) collective-permute-start(bf16[2816,256]{1,0:T(8,128)(2,1)} %copy-done.1), channel_id=1, source_target_pairs={{0,1},{1,0},{2,3},{3,2},{4,7},{5,6},{6,5},{7,4},{8,11},{9,10},{10,... | collective-permute-start | bytes 4325384 | tf_op jit(solution)/shard_map/ppermute | solution.py:85
  34.4 1.7 %collective-permute-done.3.q_other = bf16[64,2048]{1,0:T(8,128)(2,1)S(1)} collective-permute-done((bf16[64,2048]{1,0:T(8,128)(2,1)}, bf16[64,2048]{1,0:T(8,128)(2,1)S(1)}, u32[]{:S(2)}, u32[]{:S(2)}) %collective-permute-start.3) | collective-permute-done | bytes 262176 | tf_op jit(solution)/shard_map/ppermute | solution.py:89
  36.1 0.7 copy-done.7
  36.8 1.3 %copy-done.3 = bf16[848,768]{1,0:T(8,128)(2,1)S(1)} copy-done((bf16[848,768]{1,0:T(8,128)(2,1)S(1)}, bf16[848,768]{1,0:T(8,128)(2,1)}, u32[]{:S(2)}) %copy-start.3) | copy-done | bytes 1302552
  38.2 0.9 copy-done.6
  39.1 0.9 copy-done.8
  40.1 2.3 %shard_map.94 = (bf16[64,2048]{1,0:T(8,128)(2,1)S(1)}, bf16[768,768]{1,0:T(8,128)(2,1)S(1)}, bf16[768,64]{1,0:T(8,128)(2,1)S(1)}, f32[64,128]{1,0:T(8,128)S(1)}) custom-call(s32[2]{0:T(128)S(1)} %pad_add_fusion.home_ref, bf16[64,2048]{1,0:T(8,128)(2,1)S(1)} %copy-done.6, bf16[64,2048]{1,0:T(8,128)(2,1)S(1)} %copy-done.8, bf16[848,768]{1,0:T(8,128)(2,1)S(1)} %copy-done.3, ...), custom_call_target="tpu_custom_call" | custom-call | flops 75497472 | bytes 5242880 | tf_op jit(solution)/shard_map/pallas_call | solution.py:216
  42.4 1.0 copy-done.4
  43.4 1.0 collective-permute-done.1.refs_0_
  44.4 4.3 %collective-permute-start.6 = (bf16[2816,256]{1,0:T(8,128)(2,1)S(1)}, bf16[2816,256]{1,0:T(8,128)(2,1)}, u32[]{:S(2)}, u32[]{:S(2)}) collective-permute-start(bf16[2816,256]{1,0:T(8,128)(2,1)S(1)} %collective-permute-done.1.refs_0_), channel_id=1, source_target_pairs={{4,5},{5,4},{6,7},{7,6},{8,9},{9,8},{10,11},{11,10},{20,21},{21,20... | collective-permute-start | bytes 4325384 | tf_op jit(solution)/shard_map/ppermute | solution.py:85
  48.7 15.8 %collective-permute-done.5.refs_1_ = bf16[2816,256]{1,0:T(8,128)(2,1)S(1)} collective-permute-done((bf16[2816,256]{1,0:T(8,128)(2,1)}, bf16[2816,256]{1,0:T(8,128)(2,1)S(1)}, u32[]{:S(2)}, u32[]{:S(2)}) %collective-permute-start.5) | collective-permute-done | bytes 1441824 | tf_op jit(solution)/shard_map/ppermute | solution.py:85
  64.5 1.9 %collective-permute-start.9 = (bf16[2816,256]{1,0:T(8,128)(2,1)S(1)}, bf16[2816,256]{1,0:T(8,128)(2,1)}, u32[]{:S(2)}, u32[]{:S(2)}) collective-permute-start(bf16[2816,256]{1,0:T(8,128)(2,1)S(1)} %collective-permute-done.5.refs_1_), channel_id=1, source_target_pairs={{4,5},{5,4},{6,7},{7,6},{8,9},{9,8},{10,11},{11,10},{20,21},{21,20... | collective-permute-start | bytes 4325384 | tf_op jit(solution)/shard_map/ppermute | solution.py:85
  66.6 1.3 %copy-done.5 = bf16[768,768]{1,0:T(8,128)(2,1)S(1)} copy-done((bf16[768,768]{1,0:T(8,128)(2,1)S(1)}, bf16[768,768]{1,0:T(8,128)(2,1)}, u32[]{:S(2)}) %copy-start.5) | copy-done | bytes 1179672
  67.8 8.0 %shard_map.96 = (f32[256,8]{1,0:T(8,128)S(1)}, bf16[256,2048]{1,0:T(8,128)(2,1)S(1)}, bf16[256,768]{1,0:T(8,128)(2,1)S(1)}, bf16[2,6144,256]{2,1,0:T(8,128)(2,1)S(1)}) custom-call(s32[2]{0:T(128)S(1)} %pad_add_fusion.home_ref, bf16[64,4,2816]{2,1,0:T(4,128)(2,1)} %all-to-all-done.rows, bf16[768,768]{1,0:T(8,128)(2,1)S(1)} %copy-done.5, ...), custom_call_target="tpu_custom_call" | custom-call | flops 2 | bytes 2 | tf_op jit(solution)/shard_map/pallas_call | solution.py:371
  76.4 2.7 %collective-permute-done.8.u_ref = bf16[256,768]{1,0:T(8,128)(2,1)S(1)} collective-permute-done((bf16[256,768]{1,0:T(8,128)(2,1)S(1)}, bf16[256,768]{1,0:T(8,128)(2,1)S(1)}, u32[]{:S(2)}, u32[]{:S(2)}) %collective-permute-start.8) | collective-permute-done | bytes 393248 | tf_op jit(solution)/shard_map/ppermute | solution.py:89
  79.1 3.2 %shard_map.97 = (f32[256,8]{1,0:T(8,128)S(1)}, bf16[512,2048]{1,0:T(8,128)(2,1)S(1)}, bf16[512,768]{1,0:T(8,128)(2,1)S(1)}) custom-call(bf16[256,2048]{1,0:T(8,128)(2,1)S(1)} %get-tuple-element.42.acts_a, bf16[256,768]{1,0:T(8,128)(2,1)S(1)} %get-tuple-element.43.u_a, bf16[256,2048]{1,0:T(8,128)(2,1)S(1)} %collective-permute-done.7.acts, ...), custom_call_target="tpu_custom_call" | custom-call | flops 2 | bytes 2 | tf_op jit(solution)/shard_map/pallas_call | solution.py:392
  82.3 6.3 %shard_map.98 = (f32[256,8]{1,0:T(8,128)S(1)}, f32[256,8]{1,0:T(8,128)S(1)}) custom-call(s32[2]{0:T(128)S(1)} %pad_add_fusion.home_ref, bf16[512,2048]{1,0:T(8,128)(2,1)S(1)} %get-tuple-element.45.acts, bf16[512,768]{1,0:T(8,128)(2,1)S(1)} %get-tuple-element.46.u_ref, bf16[768,64]{1,0:T(8,128)(2,1)S(1)} %get-tuple-element.36.qu_ref, ...), custom_call_target="tpu_custom_call" | custom-call | flops 1 | bytes 1 | tf_op jit(solution)/shard_map/pallas_call | solution.py:414
  88.7 7.0 %shard_map.99 = f32[2,256,8]{2,1,0:T(8,128)} custom-call(s32[2]{0:T(128)S(1)} %pad_add_fusion.home_ref, bf16[512,2048]{1,0:T(8,128)(2,1)S(1)} %get-tuple-element.45.acts, bf16[512,768]{1,0:T(8,128)(2,1)S(1)} %get-tuple-element.46.u_ref, bf16[768,64]{1,0:T(8,128)(2,1)S(1)} %get-tuple-element.36.qu_ref, f32[64,128]{1,0:T(8,128)S(1)} %get-tuple-element.37.ids_ref, ...), custom_call_target="tpu_custom_call" | custom-call | flops 1 | bytes 1 | tf_op jit(solution)/shard_map/pallas_call | solution.py:414
  95.7 12.1 %all-to-all-start.1 = ((f32[128,4,8]{2,1,0:T(4,128)}), f32[128,4,8]{2,1,0:T(4,128)S(1)}, u32[]{:S(2)}, u32[]{:S(2)}) async-start(f32[128,4,8]{2,1,0:T(4,128)} %bitcast.3), calls=%async_computation.1 | async-start | bytes 524288 | tf_op jit(solution)/shard_map/all_to_all | solution.py:475
  107.8 13.8 %all-to-all-done.1 = f32[128,4,8]{2,1,0:T(4,128)S(1)} async-done(((f32[128,4,8]{2,1,0:T(4,128)}), f32[128,4,8]{2,1,0:T(4,128)S(1)}, u32[]{:S(2)}, u32[]{:S(2)}) %all-to-all-start.1) | async-done | bytes 16416 | tf_op jit(solution)/shard_map/all_to_all | solution.py:475
  (30 shorter events, 2.3 us)
Async XLA Ops:
  2.2 24.3 %collective-permute-start.2 = (bf16[2816,256]{1,0:T(8,128)(2,1)}, bf16[2816,256]{1,0:T(8,128)(2,1)S(1)}, u32[]{:S(2)}, u32[]{:S(2)}) collective-permute-start(bf16[2816,256]{1,0:T(8,128)(2,1)} %shard_map.91.after), channel_id=1, source_target_pairs={{0,3},{1,2},{2,1},{3,0},{4,8},{5,9},{6,10},{7,11},{8,4},{9,5},{10,... | collective-permute-start | bytes 4325384 | tf_op jit(solution)/shard_map/ppermute | solution.py:85
  5.6 2.7 %collective-permute-start = (bf16[8,256]{1,0:T(8,128)(2,1)S(1)}, bf16[8,256]{1,0:T(8,128)(2,1)S(1)}, u32[]{:S(2)}, u32[]{:S(2)}) collective-permute-start(bf16[8,256]{1,0:T(8,128)(2,1)S(1)} %slice.12), channel_id=1, source_target_pairs={{0,8},{8,0},{1,9},{9,1},{2,10},{10,2},{3,11},{11,3},{4,12},{12,4},... | collective-permute-start | bytes 12296 | tf_op jit(solution)/shard_map/ppermute | solution.py:89
  8.3 0.6 copy-start.9
  11.1 33.3 %collective-permute-start.1 = (bf16[2816,256]{1,0:T(8,128)(2,1)}, bf16[2816,256]{1,0:T(8,128)(2,1)S(1)}, u32[]{:S(2)}, u32[]{:S(2)}) collective-permute-start(bf16[2816,256]{1,0:T(8,128)(2,1)} %shard_map.92.refs_0_), channel_id=1, source_target_pairs={{0,1},{1,0},{2,3},{3,2},{4,8},{5,9},{6,10},{7,11},{8,4},{9,5},{10,... | collective-permute-start | bytes 4325384 | tf_op jit(solution)/shard_map/ppermute | solution.py:85
  14.4 52.2 %all-to-all-start = ((bf16[64,4,2816]{2,1,0:T(4,128)(2,1)}), bf16[64,4,2816]{2,1,0:T(4,128)(2,1)}, u32[]{:S(2)}, u32[]{:S(2)}) async-start(bf16[64,4,2816]{2,1,0:T(4,128)(2,1)} %shard_map.95), calls=%async_computation | async-start | bytes 2883584 | tf_op jit(solution)/shard_map/all_to_all | solution.py:453
  26.5 1.1 copy-start.1
  30.8 6.0 %collective-permute-start.4 = (bf16[848,768]{1,0:T(8,128)(2,1)}, bf16[848,768]{1,0:T(8,128)(2,1)}, u32[]{:S(2)}, u32[]{:S(2)}) collective-permute-start(bf16[848,768]{1,0:T(8,128)(2,1)} %get-tuple-element.30.b_own), channel_id=1, source_target_pairs={{0,8},{8,0},{1,9},{9,1},{2,10},{10,2},{3,11},{11,3},{4,12},{12,4},... | collective-permute-start | bytes 3907592 | tf_op jit(solution)/shard_map/ppermute | solution.py:89
  31.8 32.6 %collective-permute-start.5 = (bf16[2816,256]{1,0:T(8,128)(2,1)}, bf16[2816,256]{1,0:T(8,128)(2,1)S(1)}, u32[]{:S(2)}, u32[]{:S(2)}) collective-permute-start(bf16[2816,256]{1,0:T(8,128)(2,1)} %copy-done.1), channel_id=1, source_target_pairs={{0,1},{1,0},{2,3},{3,2},{4,7},{5,6},{6,5},{7,4},{8,11},{9,10},{10,... | collective-permute-start | bytes 4325384 | tf_op jit(solution)/shard_map/ppermute | solution.py:85
  34.4 1.7 %collective-permute-start.3 = (bf16[64,2048]{1,0:T(8,128)(2,1)}, bf16[64,2048]{1,0:T(8,128)(2,1)S(1)}, u32[]{:S(2)}, u32[]{:S(2)}) collective-permute-start(bf16[64,2048]{1,0:T(8,128)(2,1)} %get-tuple-element.29.q_own), channel_id=1, source_target_pairs={{0,8},{8,0},{1,9},{9,1},{2,10},{10,2},{3,11},{11,3},{4,12},{12,4},... | collective-permute-start | bytes 786440 | tf_op jit(solution)/shard_map/ppermute | solution.py:89
  34.4 32.0 %copy-start.10 = (s32[1,2,32]{2,1,0:T(2,128)S(1)}, s32[1,2,32]{2,1,0:T(2,128)}, u32[]{:S(2)}) copy-start(s32[1,2,32]{2,1,0:T(2,128)} %param.11) | copy-start | bytes 772
  36.1 0.7 copy-start.7
  36.8 1.3 %copy-start.3 = (bf16[848,768]{1,0:T(8,128)(2,1)S(1)}, bf16[848,768]{1,0:T(8,128)(2,1)}, u32[]{:S(2)}) copy-start(bf16[848,768]{1,0:T(8,128)(2,1)} %get-tuple-element.30.b_own) | copy-start | bytes 3907588
  38.2 0.9 copy-start.6
  39.1 0.9 copy-start.8
  42.4 1.0 copy-start.4
  44.4 31.4 %collective-permute-start.6 = (bf16[2816,256]{1,0:T(8,128)(2,1)S(1)}, bf16[2816,256]{1,0:T(8,128)(2,1)}, u32[]{:S(2)}, u32[]{:S(2)}) collective-permute-start(bf16[2816,256]{1,0:T(8,128)(2,1)S(1)} %collective-permute-done.1.refs_0_), channel_id=1, source_target_pairs={{4,5},{5,4},{6,7},{7,6},{8,9},{9,8},{10,11},{11,10},{20,21},{21,20... | collective-permute-start | bytes 4325384 | tf_op jit(solution)/shard_map/ppermute | solution.py:85
  64.5 24.2 %collective-permute-start.9 = (bf16[2816,256]{1,0:T(8,128)(2,1)S(1)}, bf16[2816,256]{1,0:T(8,128)(2,1)}, u32[]{:S(2)}, u32[]{:S(2)}) collective-permute-start(bf16[2816,256]{1,0:T(8,128)(2,1)S(1)} %collective-permute-done.5.refs_1_), channel_id=1, source_target_pairs={{4,5},{5,4},{6,7},{7,6},{8,9},{9,8},{10,11},{11,10},{20,21},{21,20... | collective-permute-start | bytes 4325384 | tf_op jit(solution)/shard_map/ppermute | solution.py:85
  66.6 1.3 %copy-start.5 = (bf16[768,768]{1,0:T(8,128)(2,1)S(1)}, bf16[768,768]{1,0:T(8,128)(2,1)}, u32[]{:S(2)}) copy-start(bf16[768,768]{1,0:T(8,128)(2,1)} %copy-done.4) | copy-start | bytes 3538948
  75.8 3.3 %collective-permute-start.7 = (bf16[256,2048]{1,0:T(8,128)(2,1)S(1)}, bf16[256,2048]{1,0:T(8,128)(2,1)S(1)}, u32[]{:S(2)}, u32[]{:S(2)}) collective-permute-start(bf16[256,2048]{1,0:T(8,128)(2,1)S(1)} %get-tuple-element.42.acts_a), channel_id=1, source_target_pairs={{0,8},{8,0},{1,9},{9,1},{2,10},{10,2},{3,11},{11,3},{4,12},{12,4},... | collective-permute-start | bytes 3145736 | tf_op jit(solution)/shard_map/ppermute | solution.py:89
  75.9 3.2 %collective-permute-start.8 = (bf16[256,768]{1,0:T(8,128)(2,1)S(1)}, bf16[256,768]{1,0:T(8,128)(2,1)S(1)}, u32[]{:S(2)}, u32[]{:S(2)}) collective-permute-start(bf16[256,768]{1,0:T(8,128)(2,1)S(1)} %get-tuple-element.43.u_a), channel_id=1, source_target_pairs={{0,8},{8,0},{1,9},{9,1},{2,10},{10,2},{3,11},{11,3},{4,12},{12,4},... | collective-permute-start | bytes 1179656 | tf_op jit(solution)/shard_map/ppermute | solution.py:89
  79.1 3.2 %copy-start = (bf16[2816,256]{1,0:T(8,128)(2,1)S(1)}, bf16[2816,256]{1,0:T(8,128)(2,1)}, u32[]{:S(2)}) copy-start(bf16[2816,256]{1,0:T(8,128)(2,1)} %shard_map.92.refs_0_) | copy-start | bytes 4325380
  82.3 6.4 %copy-start.2 = (bf16[2816,256]{1,0:T(8,128)(2,1)S(1)}, bf16[2816,256]{1,0:T(8,128)(2,1)}, u32[]{:S(2)}) copy-start(bf16[2816,256]{1,0:T(8,128)(2,1)} %copy-done.1) | copy-start | bytes 4325380
  95.7 25.9 %all-to-all-start.1 = ((f32[128,4,8]{2,1,0:T(4,128)}), f32[128,4,8]{2,1,0:T(4,128)S(1)}, u32[]{:S(2)}, u32[]{:S(2)}) async-start(f32[128,4,8]{2,1,0:T(4,128)} %bitcast.3), calls=%async_computation.1 | async-start | bytes 524288 | tf_op jit(solution)/shard_map/all_to_all | solution.py:475

commit v4 on v1

--- a/solution.py
+++ b/solution.py
@@ -298,15 +298,17 @@
     )
 
 
-def late_kernel(acts, u_ref, kept, *refs):
+def late_kernel(acts_a, u_a, acts, u_ref, kept, *refs):
     n_blocks = kept.shape[0]
-    sent_ref, held, sems = refs[n_blocks:]
+    sent_ref, acts_all, u_all, held, sems = refs[n_blocks:]
     copies = [
         pltpu.make_async_copy(ref.at[pl.ds(0, HIDDEN_SIZE)], held.at[n], sems.at[n])
         for n, ref in enumerate(refs[:n_blocks])
     ]
     for each in copies:
         each.start()
+    acts_all[:256], acts_all[256:] = acts_a[...], acts[...]
+    u_all[:256], u_all[256:] = u_a[...], u_ref[...]
     total = jnp.zeros((256, QUERIES), jnp.float32)
     for n, each in enumerate(copies):
         each.wait()
@@ -319,14 +321,12 @@
 
 
 def score_kernel(
-    choice, home_ref, acts_a, u_a, acts_b, u_b, qu_ref, ids_ref, q_acts, mine_in, sent_in, *refs
+    choice, home_ref, acts, u_ref, qu_ref, ids_ref, q_acts, mine_in, sent_in, *refs
 ):
     count = sum(choice)
-    mine_ref, sent_ref, held, acts, u_ref, sems = refs[count:]
+    mine_ref, sent_ref, held, sems = refs[count:]
     home = home_ref[0] == 1
     plan = fetch_blocks(home, choice, refs[:count], held, sems)
-    acts[:256], acts[256:] = acts_a[...], acts_b[...]
-    u_ref[:256], u_ref[256:] = u_a[...], u_b[...]
     total = jnp.concatenate([mine_in[...], sent_in[...]], axis=0)
     total = add_blocks(home, plan, held, acts, u_ref, qu_ref, ids_ref, q_acts, total)
     mine_ref[...] = total[:256]
@@ -367,20 +367,24 @@
     )(home, rows, b_out, *queries, *flat)
 
 
-def score_late(acts, u, kept, blocks):
+def score_late(acts_a, u_a, acts_b, u_b, kept, blocks):
     n = len(blocks)
     return pl.pallas_call(
         late_kernel,
-        out_shape=HALF,
-        in_specs=[VMEM] * 3 + [ANY] * n,
-        out_specs=VMEM,
+        out_shape=[
+            HALF,
+            jax.ShapeDtypeStruct((512, HIDDEN_SIZE), jnp.bfloat16),
+            jax.ShapeDtypeStruct((512, INNER), jnp.bfloat16),
+        ],
+        in_specs=[VMEM] * 5 + [ANY] * n,
+        out_specs=[VMEM] * 3,
         scratch_shapes=[
             pltpu.VMEM((n, HIDDEN_SIZE, 256), jnp.bfloat16),
             pltpu.SemaphoreType.DMA((n,)),
         ],
         compiler_params=pltpu.CompilerParams(vmem_limit_bytes=24 << 20),
         cost_estimate=score_cost(n),
-    )(acts, u, kept, *blocks)
+    )(acts_a, u_a, acts_b, u_b, kept, *blocks)
 
 
 def score(home, rows, queries, mine_sum, sent, blocks):
@@ -390,12 +394,10 @@
     return pl.pallas_call(
         functools.partial(score_kernel, choice),
         out_shape=[HALF, HALF],
-        in_specs=[SMEM] + [VMEM] * 9 + [ANY] * len(flat),
+        in_specs=[SMEM] + [VMEM] * 7 + [ANY] * len(flat),
         out_specs=[VMEM] * 2,
         scratch_shapes=[
             pltpu.VMEM((n, HIDDEN_SIZE + INNER, 256), jnp.bfloat16),
-            pltpu.VMEM((512, HIDDEN_SIZE), jnp.bfloat16),
-            pltpu.VMEM((512, INNER), jnp.bfloat16),
             pltpu.SemaphoreType.DMA((n,)),
         ],
         compiler_params=pltpu.CompilerParams(vmem_limit_bytes=24 << 20),
@@ -441,8 +443,8 @@
     )
     acts_a, u_a, fourth = lax.optimization_barrier((acts_a, u_a, fourth))
     acts_b, u_b = other_core(acts_a), other_core(u_a)
-    sent = score_late(acts_b, u_b, kept, [second, third])
-    rows = (acts_a, u_a, acts_b, u_b)
+    sent, acts, u = score_late(acts_a, u_a, acts_b, u_b, kept, [second, third])
+    rows = (acts, u)
     for blocks in ([[(own,), (fourth,)]], [[(first,), (fifth,)]]):
         mine_sum, sent = score(home, rows, queries, mine_sum, sent, blocks)
     mine_sum = mine_sum + other_core(sent)

time: 119 us -> 119 us (level)
    pallas_call x1, Pallas kernels: 6.69 us -> 7.9 us  [score_early(): pl.pallas_call(functools.partial(early_kernel, choice), out_shape=[HALF,...]
  transfers between devices with their start and end apart: 13 -> 13, of which waited for: 7 -> 7; matrix products, arithmetic and copies ran while one was open for 1% -> 1% of each run, Pallas kernels for 22% -> 23%
where the time goes in v4:
time: 119 us; the launch traced here: 118 us
  starting transfers between devices  39.1 us (33%)
  Pallas kernels  34.6 us (29%)
  waiting for transfers between devices  34.3 us (29%)
  local copies, waits for them, and re-layouts  9.36 us (8%)
    ppermute x5, waiting for transfers between devices, send(): return lax.ppermute(x, ('core', 'xl', 'y'), moves(home_step, guest_step))  17.3 us
    ppermute x5, starting transfers between devices, send(): return lax.ppermute(x, ('core', 'xl', 'y'), moves(home_step, guest_step))  12.1 us
    all_to_all x1, starting transfers between devices, on_device(): lax.all_to_all(rows, AXES, 0, 0, axis_index_groups=groups, tiled=True)  12.1 us
    pallas_call x2, Pallas kernels, score(): pl.pallas_call(functools.partial(score_kernel, choice), out_shape=[HALF,...  11.6 us
    all_to_all x1, starting transfers between devices, on_device(): lax.all_to_all(mine_sum.reshape(64, SLOTS, QUERIES), AXES, 0, 0, axis_ind...  11.2 us
    all_to_all x1, waiting for transfers between devices, on_device(): lax.all_to_all(mine_sum.reshape(64, SLOTS, QUERIES), AXES, 0, 0, axis_ind...  10.5 us
    pallas_call x1, Pallas kernels, score_early(): pl.pallas_call(functools.partial(early_kernel, choice), out_shape=[HALF,...  7.9 us
    unnamed x22, local copies, waits for them, and re-layouts  7.9 us
  transfers between devices with their start and end apart: 13, of which 7 were waited for; matrix products, arithmetic and copies ran while one was open for 1% of the time, Pallas kernels for 23%

profile of v4, /device:TPU:1, one launch (start us, length us, event | category | flops | bytes accessed | tf_op | source)
XLA Modules:
  0.0 118.5 jit_solution(4586257955444890823)
XLA Ops:
  0.0 2.2 %shard_map.91.after = bf16[2816,256]{1,0:T(8,128)(2,1)} custom-call(s32[1]{0:T(128)S(6)} %sub.8.which_ref, bf16[2,1,2048,256]{3,2,1,0:T(8,128)(2,1)} %basis.3, bf16[2,1,768,256]{3,2,1,0:T(8,128)(2,1)} %eigen.3, s32[1]{0:T(128)} %bitcast.1.after.which_ref.turn_ref), custom_call_target="tpu_custom_call" | custom-call | tf_op jit(solution)/shard_map/pallas_call | solution.py:146
  2.2 2.7 %collective-permute-start.1 = (bf16[2816,256]{1,0:T(8,128)(2,1)}, bf16[2816,256]{1,0:T(8,128)(2,1)S(1)}, u32[]{:S(2)}, u32[]{:S(2)}) collective-permute-start(bf16[2816,256]{1,0:T(8,128)(2,1)} %shard_map.91.after), channel_id=1, source_target_pairs={{0,3},{1,2},{2,1},{3,0},{4,8},{5,9},{6,10},{7,11},{8,4},{9,5},{10,... | collective-permute-start | bytes 4325384 | tf_op jit(solution)/shard_map/ppermute | solution.py:71
  5.6 1.9 %collective-permute-start = (bf16[8,256]{1,0:T(8,128)(2,1)S(1)}, bf16[8,256]{1,0:T(8,128)(2,1)S(1)}, u32[]{:S(2)}, u32[]{:S(2)}) collective-permute-start(bf16[8,256]{1,0:T(8,128)(2,1)S(1)} %slice.4), channel_id=1, source_target_pairs={{0,8},{8,0},{1,9},{9,1},{2,10},{10,2},{3,11},{11,3},{4,12},{12,4},... | collective-permute-start | bytes 12296 | tf_op jit(solution)/shard_map/ppermute | solution.py:75
  7.5 0.8 collective-permute-done.after
  8.9 2.2 %shard_map.93.refs_0_ = bf16[2816,256]{1,0:T(8,128)(2,1)} custom-call(s32[1]{0:T(128)} %bitcast.1.after.which_ref.turn_ref, bf16[2,1,2048,256]{3,2,1,0:T(8,128)(2,1)} %basis.3, bf16[2,1,768,256]{3,2,1,0:T(8,128)(2,1)} %eigen.3, bf16[8,256]{1,0:T(8,128)(2,1)} %copy-done.9), custom_call_target="tpu_custom_call" | custom-call | tf_op jit(solution)/shard_map/pallas_call | solution.py:146
  11.1 0.7 collective-permute-start.4
  11.8 2.6 %shard_map.92 = bf16[64,4,2816]{2,1,0:T(4,128)(2,1)} custom-call(bf16[256,2048]{1,0:T(8,128)(2,1)} %acts.1, bf16[256,768]{1,0:T(8,128)(2,1)} %grads.1, bf16[2816,256]{1,0:T(8,128)(2,1)} %shard_map.91.after), custom_call_target="tpu_custom_call" | custom-call | tf_op jit(solution)/shard_map/pallas_call | solution.py:175
  14.4 12.1 %all-to-all-start = ((bf16[64,4,2816]{2,1,0:T(4,128)(2,1)}), bf16[64,4,2816]{2,1,0:T(4,128)(2,1)}, u32[]{:S(2)}, u32[]{:S(2)}) async-start(bf16[64,4,2816]{2,1,0:T(4,128)(2,1)} %shard_map.92), calls=%async_computation | async-start | bytes 2883584 | tf_op jit(solution)/shard_map/all_to_all | solution.py:433
  26.5 1.1 copy-done
  27.6 3.2 %shard_map.94 = (bf16[64,2048]{1,0:T(8,128)(2,1)}, bf16[848,768]{1,0:T(8,128)(2,1)}) custom-call(s32[1]{0:T(128)} %bitcast.1.after.which_ref.turn_ref, s32[2,1,64]{2,1,0:T(1,128)} %ids.1, bf16[2,1,64,2048]{3,2,1,0:T(8,128)(2,1)} %q_acts.1, bf16[2,1,64,768]{3,2,1,0:T(8,128)(2,1)} %q_grads.1, bf16[2,1,768,768]{3,2,1,0:T(8,128)(2,1)} %b_out.1, ...), custom_call_target="tpu_custom_call" | custom-call | tf_op jit(solution)/shard_map/pallas_call | solution.py:157
  30.9 1.0 collective-permute-start.3
  31.9 2.5 %collective-permute-start.5 = (bf16[2816,256]{1,0:T(8,128)(2,1)}, bf16[2816,256]{1,0:T(8,128)(2,1)S(1)}, u32[]{:S(2)}, u32[]{:S(2)}) collective-permute-start(bf16[2816,256]{1,0:T(8,128)(2,1)} %copy-done), channel_id=1, source_target_pairs={{0,1},{1,0},{2,3},{3,2},{4,7},{5,6},{6,5},{7,4},{8,11},{9,10},{10,... | collective-permute-start | bytes 4325384 | tf_op jit(solution)/shard_map/ppermute | solution.py:71
  34.4 1.7 %collective-permute-done.2.q_other = bf16[64,2048]{1,0:T(8,128)(2,1)S(1)} collective-permute-done((bf16[64,2048]{1,0:T(8,128)(2,1)}, bf16[64,2048]{1,0:T(8,128)(2,1)S(1)}, u32[]{:S(2)}, u32[]{:S(2)}) %collective-permute-start.2) | collective-permute-done | bytes 262176 | tf_op jit(solution)/shard_map/ppermute | solution.py:75
  36.2 0.7 copy-done.7
  36.9 1.3 %copy-done.3 = bf16[848,768]{1,0:T(8,128)(2,1)S(1)} copy-done((bf16[848,768]{1,0:T(8,128)(2,1)S(1)}, bf16[848,768]{1,0:T(8,128)(2,1)}, u32[]{:S(2)}) %copy-start.3) | copy-done | bytes 1302552
  38.2 0.9 copy-done.6
  39.1 0.9 copy-done.8
  40.1 1.8 %shard_map.95 = (bf16[64,2048]{1,0:T(8,128)(2,1)S(1)}, bf16[768,768]{1,0:T(8,128)(2,1)S(1)}, bf16[768,64]{1,0:T(8,128)(2,1)S(1)}, f32[64,128]{1,0:T(8,128)S(1)}) custom-call(s32[1]{0:T(128)} %bitcast.home_ref, bf16[64,2048]{1,0:T(8,128)(2,1)S(1)} %copy-done.6, bf16[64,2048]{1,0:T(8,128)(2,1)S(1)} %copy-done.8, bf16[848,768]{1,0:T(8,128)(2,1)S(1)} %copy-done.3, ...), custom_call_target="tpu_custom_call" | custom-call | flops 75497472 | bytes 5242880 | tf_op jit(solution)/shard_map/pallas_call | solution.py:202
  41.9 1.0 copy-done.4
  42.9 1.5 %collective-permute-done.4.refs_0_ = bf16[2816,256]{1,0:T(8,128)(2,1)S(1)} collective-permute-done((bf16[2816,256]{1,0:T(8,128)(2,1)}, bf16[2816,256]{1,0:T(8,128)(2,1)S(1)}, u32[]{:S(2)}, u32[]{:S(2)}) %collective-permute-start.4) | collective-permute-done | bytes 1441824 | tf_op jit(solution)/shard_map/ppermute | solution.py:71
  44.4 4.3 %collective-permute-start.6 = (bf16[2816,256]{1,0:T(8,128)(2,1)S(1)}, bf16[2816,256]{1,0:T(8,128)(2,1)}, u32[]{:S(2)}, u32[]{:S(2)}) collective-permute-start(bf16[2816,256]{1,0:T(8,128)(2,1)S(1)} %collective-permute-done.4.refs_0_), channel_id=1, source_target_pairs={{4,5},{5,4},{6,7},{7,6},{8,9},{9,8},{10,11},{11,10},{20,21},{21,20... | collective-permute-start | bytes 4325384 | tf_op jit(solution)/shard_map/ppermute | solution.py:71
  48.7 15.8 %collective-permute-done.5.refs_1_ = bf16[2816,256]{1,0:T(8,128)(2,1)S(1)} collective-permute-done((bf16[2816,256]{1,0:T(8,128)(2,1)}, bf16[2816,256]{1,0:T(8,128)(2,1)S(1)}, u32[]{:S(2)}, u32[]{:S(2)}) %collective-permute-start.5) | collective-permute-done | bytes 1441824 | tf_op jit(solution)/shard_map/ppermute | solution.py:71
  64.5 1.9 %collective-permute-start.9 = (bf16[2816,256]{1,0:T(8,128)(2,1)S(1)}, bf16[2816,256]{1,0:T(8,128)(2,1)}, u32[]{:S(2)}, u32[]{:S(2)}) collective-permute-start(bf16[2816,256]{1,0:T(8,128)(2,1)S(1)} %collective-permute-done.5.refs_1_), channel_id=1, source_target_pairs={{4,5},{5,4},{6,7},{7,6},{8,9},{9,8},{10,11},{11,10},{20,21},{21,20... | collective-permute-start | bytes 4325384 | tf_op jit(solution)/shard_map/ppermute | solution.py:71
  66.4 1.3 %copy-done.5 = bf16[768,768]{1,0:T(8,128)(2,1)S(1)} copy-done((bf16[768,768]{1,0:T(8,128)(2,1)S(1)}, bf16[768,768]{1,0:T(8,128)(2,1)}, u32[]{:S(2)}) %copy-start.5) | copy-done | bytes 1179672
  67.7 7.9 %shard_map.96 = (f32[256,8]{1,0:T(8,128)S(1)}, bf16[256,2048]{1,0:T(8,128)(2,1)S(1)}, bf16[256,768]{1,0:T(8,128)(2,1)S(1)}, bf16[2,6144,256]{2,1,0:T(8,128)(2,1)S(1)}) custom-call(s32[1]{0:T(128)} %bitcast.home_ref, bf16[64,4,2816]{2,1,0:T(4,128)(2,1)} %all-to-all-done.rows, bf16[768,768]{1,0:T(8,128)(2,1)S(1)} %copy-done.5, ...), custom_call_target="tpu_custom_call" | custom-call | flops 2 | bytes 2 | tf_op jit(solution)/shard_map/pallas_call | solution.py:351
  76.2 2.7 %collective-permute-done.8.u_ref = bf16[256,768]{1,0:T(8,128)(2,1)S(1)} collective-permute-done((bf16[256,768]{1,0:T(8,128)(2,1)S(1)}, bf16[256,768]{1,0:T(8,128)(2,1)S(1)}, u32[]{:S(2)}, u32[]{:S(2)}) %collective-permute-start.8) | collective-permute-done | bytes 393248 | tf_op jit(solution)/shard_map/ppermute | solution.py:75
  78.9 3.2 %shard_map.97 = (f32[256,8]{1,0:T(8,128)S(1)}, bf16[512,2048]{1,0:T(8,128)(2,1)S(1)}, bf16[512,768]{1,0:T(8,128)(2,1)S(1)}) custom-call(bf16[256,2048]{1,0:T(8,128)(2,1)S(1)} %get-tuple-element.40.acts_a, bf16[256,768]{1,0:T(8,128)(2,1)S(1)} %get-tuple-element.41.u_a, bf16[256,2048]{1,0:T(8,128)(2,1)S(1)} %collective-permute-done.7.acts, ...), custom_call_target="tpu_custom_call" | custom-call | flops 2 | bytes 2 | tf_op jit(solution)/shard_map/pallas_call | solution.py:372
  82.1 5.9 %shard_map.98 = (f32[256,8]{1,0:T(8,128)S(1)}, f32[256,8]{1,0:T(8,128)S(1)}) custom-call(s32[1]{0:T(128)} %bitcast.home_ref, bf16[512,2048]{1,0:T(8,128)(2,1)S(1)} %get-tuple-element.43.acts, bf16[512,768]{1,0:T(8,128)(2,1)S(1)} %get-tuple-element.44.u_ref, bf16[768,64]{1,0:T(8,128)(2,1)S(1)} %get-tuple-element.34.qu_ref, ...), custom_call_target="tpu_custom_call" | custom-call | flops 1 | bytes 1 | tf_op jit(solution)/shard_map/pallas_call | solution.py:394
  88.0 5.8 %shard_map.99 = (f32[256,8]{1,0:T(8,128)S(1)}, f32[256,8]{1,0:T(8,128)S(1)}) custom-call(s32[1]{0:T(128)} %bitcast.home_ref, bf16[512,2048]{1,0:T(8,128)(2,1)S(1)} %get-tuple-element.43.acts, bf16[512,768]{1,0:T(8,128)(2,1)S(1)} %get-tuple-element.44.u_ref, bf16[768,64]{1,0:T(8,128)(2,1)S(1)} %get-tuple-element.34.qu_ref, ...), custom_call_target="tpu_custom_call" | custom-call | flops 1 | bytes 1 | tf_op jit(solution)/shard_map/pallas_call | solution.py:394
  94.0 1.2 %collective-permute-done.10 = f32[256,8]{1,0:T(8,128)S(1)} collective-permute-done((f32[256,8]{1,0:T(8,128)S(1)}, f32[256,8]{1,0:T(8,128)S(1)}, u32[]{:S(2)}, u32[]{:S(2)}) %collective-permute-start.10) | collective-permute-done | bytes 8224 | tf_op jit(solution)/shard_map/ppermute | solution.py:75
  95.9 11.2 %all-to-all-start.1 = ((f32[64,4,8]{2,1,0:T(4,128)}), f32[64,4,8]{2,1,0:T(4,128)S(1)}, u32[]{:S(2)}, u32[]{:S(2)}) async-start(f32[64,4,8]{2,1,0:T(4,128)} %bitcast.2), calls=%async_computation.1 | async-start | bytes 262144 | tf_op jit(solution)/shard_map/all_to_all | solution.py:451
  107.2 10.5 %all-to-all-done.1 = f32[64,4,8]{2,1,0:T(4,128)S(1)} async-done(((f32[64,4,8]{2,1,0:T(4,128)}), f32[64,4,8]{2,1,0:T(4,128)S(1)}, u32[]{:S(2)}, u32[]{:S(2)}) %all-to-all-start.1) | async-done | bytes 8224 | tf_op jit(solution)/shard_map/all_to_all | solution.py:451
  (31 shorter events, 3.7 us)
Async XLA Ops:
  2.2 24.3 %collective-permute-start.1 = (bf16[2816,256]{1,0:T(8,128)(2,1)}, bf16[2816,256]{1,0:T(8,128)(2,1)S(1)}, u32[]{:S(2)}, u32[]{:S(2)}) collective-permute-start(bf16[2816,256]{1,0:T(8,128)(2,1)} %shard_map.91.after), channel_id=1, source_target_pairs={{0,3},{1,2},{2,1},{3,0},{4,8},{5,9},{6,10},{7,11},{8,4},{9,5},{10,... | collective-permute-start | bytes 4325384 | tf_op jit(solution)/shard_map/ppermute | solution.py:71
  5.6 2.7 %collective-permute-start = (bf16[8,256]{1,0:T(8,128)(2,1)S(1)}, bf16[8,256]{1,0:T(8,128)(2,1)S(1)}, u32[]{:S(2)}, u32[]{:S(2)}) collective-permute-start(bf16[8,256]{1,0:T(8,128)(2,1)S(1)} %slice.4), channel_id=1, source_target_pairs={{0,8},{8,0},{1,9},{9,1},{2,10},{10,2},{3,11},{11,3},{4,12},{12,4},... | collective-permute-start | bytes 12296 | tf_op jit(solution)/shard_map/ppermute | solution.py:75
  8.3 0.6 copy-start.9
  11.1 33.3 %collective-permute-start.4 = (bf16[2816,256]{1,0:T(8,128)(2,1)}, bf16[2816,256]{1,0:T(8,128)(2,1)S(1)}, u32[]{:S(2)}, u32[]{:S(2)}) collective-permute-start(bf16[2816,256]{1,0:T(8,128)(2,1)} %shard_map.93.refs_0_), channel_id=1, source_target_pairs={{0,1},{1,0},{2,3},{3,2},{4,8},{5,9},{6,10},{7,11},{8,4},{9,5},{10,... | collective-permute-start | bytes 4325384 | tf_op jit(solution)/shard_map/ppermute | solution.py:71
  14.4 52.0 %all-to-all-start = ((bf16[64,4,2816]{2,1,0:T(4,128)(2,1)}), bf16[64,4,2816]{2,1,0:T(4,128)(2,1)}, u32[]{:S(2)}, u32[]{:S(2)}) async-start(bf16[64,4,2816]{2,1,0:T(4,128)(2,1)} %shard_map.92), calls=%async_computation | async-start | bytes 2883584 | tf_op jit(solution)/shard_map/all_to_all | solution.py:433
  26.5 1.1 copy-start
  30.9 6.0 %collective-permute-start.3 = (bf16[848,768]{1,0:T(8,128)(2,1)}, bf16[848,768]{1,0:T(8,128)(2,1)}, u32[]{:S(2)}, u32[]{:S(2)}) collective-permute-start(bf16[848,768]{1,0:T(8,128)(2,1)} %get-tuple-element.31.b_own), channel_id=1, source_target_pairs={{0,8},{8,0},{1,9},{9,1},{2,10},{10,2},{3,11},{11,3},{4,12},{12,4},... | collective-permute-start | bytes 3907592 | tf_op jit(solution)/shard_map/ppermute | solution.py:75
  31.9 32.6 %collective-permute-start.5 = (bf16[2816,256]{1,0:T(8,128)(2,1)}, bf16[2816,256]{1,0:T(8,128)(2,1)S(1)}, u32[]{:S(2)}, u32[]{:S(2)}) collective-permute-start(bf16[2816,256]{1,0:T(8,128)(2,1)} %copy-done), channel_id=1, source_target_pairs={{0,1},{1,0},{2,3},{3,2},{4,7},{5,6},{6,5},{7,4},{8,11},{9,10},{10,... | collective-permute-start | bytes 4325384 | tf_op jit(solution)/shard_map/ppermute | solution.py:71
  34.4 1.7 %collective-permute-start.2 = (bf16[64,2048]{1,0:T(8,128)(2,1)}, bf16[64,2048]{1,0:T(8,128)(2,1)S(1)}, u32[]{:S(2)}, u32[]{:S(2)}) collective-permute-start(bf16[64,2048]{1,0:T(8,128)(2,1)} %get-tuple-element.30.q_own), channel_id=1, source_target_pairs={{0,8},{8,0},{1,9},{9,1},{2,10},{10,2},{3,11},{11,3},{4,12},{12,4},... | collective-permute-start | bytes 786440 | tf_op jit(solution)/shard_map/ppermute | solution.py:75
  36.1 0.7 copy-start.7
  36.9 1.3 %copy-start.3 = (bf16[848,768]{1,0:T(8,128)(2,1)S(1)}, bf16[848,768]{1,0:T(8,128)(2,1)}, u32[]{:S(2)}) copy-start(bf16[848,768]{1,0:T(8,128)(2,1)} %get-tuple-element.31.b_own) | copy-start | bytes 3907588
  38.2 0.9 copy-start.6
  39.1 0.9 copy-start.8
  41.9 1.0 copy-start.4
  44.4 31.2 %collective-permute-start.6 = (bf16[2816,256]{1,0:T(8,128)(2,1)S(1)}, bf16[2816,256]{1,0:T(8,128)(2,1)}, u32[]{:S(2)}, u32[]{:S(2)}) collective-permute-start(bf16[2816,256]{1,0:T(8,128)(2,1)S(1)} %collective-permute-done.4.refs_0_), channel_id=1, source_target_pairs={{4,5},{5,4},{6,7},{7,6},{8,9},{9,8},{10,11},{11,10},{20,21},{21,20... | collective-permute-start | bytes 4325384 | tf_op jit(solution)/shard_map/ppermute | solution.py:71
  64.5 23.5 %collective-permute-start.9 = (bf16[2816,256]{1,0:T(8,128)(2,1)S(1)}, bf16[2816,256]{1,0:T(8,128)(2,1)}, u32[]{:S(2)}, u32[]{:S(2)}) collective-permute-start(bf16[2816,256]{1,0:T(8,128)(2,1)S(1)} %collective-permute-done.5.refs_1_), channel_id=1, source_target_pairs={{4,5},{5,4},{6,7},{7,6},{8,9},{9,8},{10,11},{11,10},{20,21},{21,20... | collective-permute-start | bytes 4325384 | tf_op jit(solution)/shard_map/ppermute | solution.py:71
  66.4 1.3 %copy-start.5 = (bf16[768,768]{1,0:T(8,128)(2,1)S(1)}, bf16[768,768]{1,0:T(8,128)(2,1)}, u32[]{:S(2)}) copy-start(bf16[768,768]{1,0:T(8,128)(2,1)} %copy-done.4) | copy-start | bytes 3538948
  75.6 3.3 %collective-permute-start.7 = (bf16[256,2048]{1,0:T(8,128)(2,1)S(1)}, bf16[256,2048]{1,0:T(8,128)(2,1)S(1)}, u32[]{:S(2)}, u32[]{:S(2)}) collective-permute-start(bf16[256,2048]{1,0:T(8,128)(2,1)S(1)} %get-tuple-element.40.acts_a), channel_id=1, source_target_pairs={{0,8},{8,0},{1,9},{9,1},{2,10},{10,2},{3,11},{11,3},{4,12},{12,4},... | collective-permute-start | bytes 3145736 | tf_op jit(solution)/shard_map/ppermute | solution.py:75
  75.7 3.2 %collective-permute-start.8 = (bf16[256,768]{1,0:T(8,128)(2,1)S(1)}, bf16[256,768]{1,0:T(8,128)(2,1)S(1)}, u32[]{:S(2)}, u32[]{:S(2)}) collective-permute-start(bf16[256,768]{1,0:T(8,128)(2,1)S(1)} %get-tuple-element.41.u_a), channel_id=1, source_target_pairs={{0,8},{8,0},{1,9},{9,1},{2,10},{10,2},{3,11},{11,3},{4,12},{12,4},... | collective-permute-start | bytes 1179656 | tf_op jit(solution)/shard_map/ppermute | solution.py:75
  78.9 3.2 %copy-start.2 = (bf16[2816,256]{1,0:T(8,128)(2,1)S(1)}, bf16[2816,256]{1,0:T(8,128)(2,1)}, u32[]{:S(2)}) copy-start(bf16[2816,256]{1,0:T(8,128)(2,1)} %shard_map.93.refs_0_) | copy-start | bytes 4325380
  82.1 5.9 %copy-start.1 = (bf16[2816,256]{1,0:T(8,128)(2,1)S(1)}, bf16[2816,256]{1,0:T(8,128)(2,1)}, u32[]{:S(2)}) copy-start(bf16[2816,256]{1,0:T(8,128)(2,1)} %copy-done) | copy-start | bytes 4325380
  88.0 5.9 %copy-start.10 = (s32[1,2,32]{2,1,0:T(2,128)S(1)}, s32[1,2,32]{2,1,0:T(2,128)}, u32[]{:S(2)}) copy-start(s32[1,2,32]{2,1,0:T(2,128)} %param.11) | copy-start | bytes 772
  93.8 1.4 %collective-permute-start.10 = (f32[256,8]{1,0:T(8,128)S(1)}, f32[256,8]{1,0:T(8,128)S(1)}, u32[]{:S(2)}, u32[]{:S(2)}) collective-permute-start(f32[256,8]{1,0:T(8,128)S(1)} %get-tuple-element.52), channel_id=1, source_target_pairs={{0,8},{8,0},{1,9},{9,1},{2,10},{10,2},{3,11},{11,3},{4,12},{12,4},... | collective-permute-start | bytes 24584 | tf_op jit(solution)/shard_map/ppermute | solution.py:75
  95.9 21.8 %all-to-all-start.1 = ((f32[64,4,8]{2,1,0:T(4,128)}), f32[64,4,8]{2,1,0:T(4,128)S(1)}, u32[]{:S(2)}, u32[]{:S(2)}) async-start(f32[64,4,8]{2,1,0:T(4,128)} %bitcast.2), calls=%async_computation.1 | async-start | bytes 262144 | tf_op jit(solution)/shard_map/all_to_all | solution.py:451
